TPU v7x, 256 devices: a whole 4x4x8 slice. The times are simulated.
256 devices in a mesh: seg: 8 (over x, core), blk: 32 (over z, y).
Axes of the slice: x: 4, y: 4, z: 8, core: 2. Of those that a mesh axis runs over, the one named last changes fastest.
Arguments:
- guess_blocks: bfloat16 [8, 32, 512, 512], P('seg', 'blk'), may hold values from -180 to 180, as said below
- onsite_left: bfloat16 [8, 32, 2, 512, 512], P('seg', 'blk'), may hold values from -0.375 to 1.375, as said below
- onsite_right: bfloat16 [8, 32, 2, 512, 512], P('seg', 'blk'), may hold values from -0.375 to 1.375, as said below
- hopping_left: bfloat16 [8, 32, 512, 512], P('seg', 'blk'), may hold values from -0.25 to 0.25
- hopping_right: bfloat16 [8, 32, 512, 512], P('seg', 'blk'), may hold values from -0.25 to 0.25
- sector_dims: int32 [8, 32, 2], P('seg', 'blk'), may hold values from 192 to 512, as said below
- kept_dims: int32 [8, 32], P('seg', 'blk'), may hold values from 64 to 512, as said below
Outputs:
- ground_blocks: float32 [8, 32, 512, 512], P('seg', 'blk')
- energy: float32 [8], P('seg')
- left_environment: bfloat16 [8, 32, 512, 512], P('seg', 'blk')
- right_environment: bfloat16 [8, 32, 512, 512], P('seg', 'blk')
Inputs may be any that keep to these rules, and one draw needn't show every extreme that they name: guess_blocks is drawn independently of the other arrays. Each onsite_left[g, s, k] is a symmetric matrix. Each onsite_right[g, s, k] is a symmetric matrix. `sector_dims`: every entry is a multiple of 64; in every segment some sector has 512 live rows and some sector 512 live columns. `kept_dims`: every entry is a multiple of 64; in every segment some sector keeps 512.
All inputs are finite; a program needn't handle non-finite values.
Results may differ from a plain program's by a relative error of at most 0.015.
Values may be sent and summed in bfloat16 or wider, within the bound.
A program may use at most 64 MiB of HBM per device.

v0:
```python
import math

import jax
import jax.numpy as jnp
from jax import lax
from jax.sharding import PartitionSpec as P

ITERS = 4


def shifted(block, axis, distance):
    devices = range(lax.axis_size(axis))
    route = [(i - distance, i) for i in devices if i - distance in devices]
    return lax.ppermute(block, axis, route)


def per_device(
    guess_blocks, onsite_left, onsite_right, hopping_left, hopping_right, sector_dims, kept_dims
):
    left_factors = onsite_left[0]
    right_factors = onsite_right[0]
    hop_left = hopping_left[0]
    hop_right = hopping_right[0]
    live_dims = sector_dims[0]
    kept_sizes = kept_dims[0]
    block_width = left_factors.shape[-1]
    local_count = left_factors.shape[0]
    term_count = left_factors.shape[1]
    total_sectors = local_count * lax.axis_size("blk")
    positions = jnp.arange(block_width, dtype=jnp.int32)
    live_mask = (
        (positions[None, :, None] < live_dims[:, 0][:, None, None])
        & (positions[None, None, :] < live_dims[:, 1][:, None, None])
    ).astype(jnp.float32)

    def operator(field):
        blocks = field.astype(jnp.bfloat16)
        summed = jnp.zeros(field.shape, jnp.float32)
        for term_index in range(term_count):
            partial_left = jnp.einsum(
                "sij,sjk->sik",
                left_factors[:, term_index],
                blocks,
                preferred_element_type=jnp.float32,
            ).astype(jnp.bfloat16)
            summed = summed + jnp.einsum(
                "sij,sjk->sik",
                partial_left,
                right_factors[:, term_index],
                preferred_element_type=jnp.float32,
            )
        incoming = shifted(blocks[:1], "blk", -1)
        following = jnp.concatenate([blocks[1:], incoming], axis=0)
        partial_next = jnp.einsum(
            "sij,sjk->sik", hop_left, following, preferred_element_type=jnp.float32
        ).astype(jnp.bfloat16)
        summed = summed + jnp.einsum(
            "sij,skj->sik", partial_next, hop_right, preferred_element_type=jnp.float32
        )
        partial_prev = jnp.einsum(
            "sji,sjk->sik", hop_left, blocks, preferred_element_type=jnp.float32
        ).astype(jnp.bfloat16)
        coupled = jnp.einsum(
            "sij,sjk->sik", partial_prev, hop_right, preferred_element_type=jnp.float32
        )
        arrived = shifted(coupled[-1:].astype(jnp.bfloat16), "blk", 1).astype(jnp.float32)
        summed = summed + jnp.concatenate([arrived, coupled[:-1]], axis=0)
        return summed * live_mask

    diagonal = jnp.zeros(live_mask.shape, jnp.float32)
    for term_index in range(term_count):
        left_diag = jnp.diagonal(left_factors[:, term_index], axis1=1, axis2=2).astype(jnp.float32)
        right_diag = jnp.diagonal(right_factors[:, term_index], axis1=1, axis2=2).astype(
            jnp.float32
        )
        diagonal = diagonal + left_diag[:, :, None] * right_diag[:, None, :]
    diagonal = diagonal * live_mask
    vector = guess_blocks[0].astype(jnp.float32) * live_mask
    norm_total = lax.psum(jnp.sum(vector * vector), "blk")
    vector = vector / jnp.sqrt(norm_total)
    image = operator(vector)
    energy = lax.psum(jnp.sum(vector * image), "blk")
    for iteration in range(ITERS):
        residual = image - energy * vector
        correction = residual / (1.0 + jnp.abs(diagonal - energy))
        correlation, weight = lax.psum(
            (jnp.sum(vector * correction), jnp.sum(correction * correction)), "blk"
        )
        applied = operator(correction)
        cross_term, curvature = lax.psum(
            (jnp.sum(vector * applied), jnp.sum(correction * applied)), "blk"
        )
        span_square = weight - correlation * correlation
        length = jnp.sqrt(span_square)
        off_diagonal = (cross_term - correlation * energy) / length
        lower_value = (
            curvature - 2.0 * correlation * cross_term + correlation * correlation * energy
        ) / span_square
        half_gap = (energy - lower_value) / 2.0
        radius = jnp.sqrt(half_gap * half_gap + off_diagonal * off_diagonal)
        keep_coef = radius - half_gap
        turn_coef = -off_diagonal
        coef_norm = jnp.sqrt(keep_coef * keep_coef + turn_coef * turn_coef)
        vector = (
            keep_coef * vector + turn_coef * (correction - correlation * vector) / length
        ) / coef_norm
        image = (
            keep_coef * image + turn_coef * (applied - correlation * image) / length
        ) / coef_norm
        energy = (energy + lower_value) / 2.0 - radius
    ground = vector * (block_width * math.sqrt(total_sectors))
    final_blocks = vector.astype(jnp.bfloat16)
    kept_mask = (
        (positions[None, :, None] < kept_sizes[:, None, None])
        & (positions[None, None, :] < kept_sizes[:, None, None])
    ).astype(jnp.float32)
    handoff_scale = total_sectors * block_width * math.sqrt(block_width)
    left_part = jnp.einsum(
        "sij,sjk->sik", left_factors[:, 0], final_blocks, preferred_element_type=jnp.float32
    ).astype(jnp.bfloat16)
    outgoing_left = (
        jnp.einsum("sji,sjk->sik", final_blocks, left_part, preferred_element_type=jnp.float32)
        * handoff_scale
        * kept_mask
    ).astype(jnp.bfloat16)
    right_part = jnp.einsum(
        "sij,sjk->sik", final_blocks, right_factors[:, 0], preferred_element_type=jnp.float32
    ).astype(jnp.bfloat16)
    outgoing_right = (
        jnp.einsum("sij,skj->sik", right_part, final_blocks, preferred_element_type=jnp.float32)
        * handoff_scale
        * kept_mask
    ).astype(jnp.bfloat16)
    received_left = shifted(outgoing_left, "seg", 1)
    received_right = shifted(outgoing_right, "seg", -1)
    segment_index = lax.axis_index("seg")
    left_environment = jnp.where(segment_index == 0, left_factors[:, 0], received_left)
    right_environment = jnp.where(
        segment_index == lax.axis_size("seg") - 1, right_factors[:, 0], received_right
    )
    return (ground[None], energy.reshape(1), left_environment[None], right_environment[None])


def solution(mesh):
    in_specs = (
        P("seg", "blk", None, None),
        P("seg", "blk", None, None, None),
        P("seg", "blk", None, None, None),
        P("seg", "blk", None, None),
        P("seg", "blk", None, None),
        P("seg", "blk", None),
        P("seg", "blk"),
    )
    out_specs = (
        P("seg", "blk", None, None),
        P("seg"),
        P("seg", "blk", None, None),
        P("seg", "blk", None, None),
    )
    return jax.shard_map(
        per_device, mesh=mesh, in_specs=in_specs, out_specs=out_specs, check_vma=False
    )
```

profile of v0, /device:TPU:1, one launch (start us, length us, event | category | flops | bytes accessed | tf_op | source)
XLA Modules:
  0.0 647.0 jit_solution(7989724754558001709)
XLA Ops:
  3.2 2.1 fusion.28
  5.3 65.2 %psum.126 = f32[]{:T(128)} all-reduce(f32[]{:T(128)} %fusion.28), channel_id=1, replica_groups=mesh['seg'=8,'blk'=32] {'blk'}, use_global_device_ids=true, to_apply=%region_1.2 | all-reduce | flops 1 | bytes 8 | tf_op jit(solution)/shard_map/psum | solution.py:79
  72.3 1.4 collective-permute-start
  73.7 1.8 fusion.16
  75.5 4.8 collective-permute-start.1
  81.9 2.0 fusion.11
  84.9 8.2 %gather_fusion = bf16[512]{0:T(512)(128)(2,1)S(1)} fusion(bf16[512,512]{1,0:T(8,128)(2,1)} %get-tuple-element.50, s32[512]{0:T(512)S(1)} %bitcast.306), kind=kCustom, calls=%fused_computation | custom fusion | bytes 6144 | tf_op jit(solution)/shard_map/jit(diagonal)/gather | solution.py:72
  93.2 8.3 %gather_fusion.1 = bf16[512]{0:T(512)(128)(2,1)S(1)} fusion(bf16[512,512]{1,0:T(8,128)(2,1)} %get-tuple-element.52, s32[512]{0:T(512)S(1)} %bitcast.307), kind=kCustom, calls=%fused_computation.1 | custom fusion | bytes 6144 | tf_op jit(solution)/shard_map/jit(diagonal)/gather | solution.py:73
  101.4 8.0 %gather_fusion.2 = bf16[512]{0:T(512)(128)(2,1)S(1)} fusion(bf16[512,512]{1,0:T(8,128)(2,1)} %get-tuple-element.51, s32[512]{0:T(512)S(1)} %bitcast.308), kind=kCustom, calls=%fused_computation.2 | custom fusion | bytes 6144 | tf_op jit(solution)/shard_map/jit(diagonal)/gather | solution.py:72
  109.5 8.5 %gather_fusion.3 = bf16[512]{0:T(512)(128)(2,1)S(1)} fusion(bf16[512,512]{1,0:T(8,128)(2,1)} %get-tuple-element.53, s32[512]{0:T(512)S(1)} %bitcast.309), kind=kCustom, calls=%fused_computation.3 | custom fusion | bytes 6144 | tf_op jit(solution)/shard_map/jit(diagonal)/gather | solution.py:73
  118.6 3.2 convolution_add_fusion.9
  121.8 4.4 multiply_reduce_fusion.16
  126.3 56.4 %psum.127 = f32[]{:T(128)} all-reduce(f32[]{:T(128)} %get-tuple-element.56), channel_id=1, replica_groups=mesh['seg'=8,'blk'=32] {'blk'}, use_global_device_ids=true, to_apply=%region_3.4 | all-reduce | flops 1 | bytes 8 | tf_op jit(solution)/shard_map/psum | solution.py:82
  182.7 3.7 fusion.117
  186.3 2.9 fusion.17
  190.5 5.1 collective-permute-start.3
  195.6 2.9 fusion.12
  198.4 3.2 convolution_add_fusion.7
  201.7 5.0 multiply_reduce_fusion.12
  206.7 58.5 %all-reduce.3 = (f32[]{:T(128)}, f32[]{:T(128)}, f32[]{:T(128)}, f32[]{:T(128)}) all-reduce(f32[]{:T(128)} %get-tuple-element.18, f32[]{:T(128)} %get-tuple-element.17, f32[]{:T(128)} %get-tuple-element.19, f32[]{:T(128)} %get-tuple-element.16), channel_id=1, replica_groups=mesh['seg'=8,'blk'=32] {'blk'}, use_global_device_ids=true, to_apply=%region_5.6 | all-reduce | flops 4 | bytes 32 | tf_op jit(solution)/shard_map/psum | solution.py:90
  272.8 4.2 fusion.116
  277.0 2.8 fusion.18
  281.1 4.8 collective-permute-start.5
  285.9 2.9 fusion.13
  288.8 3.3 convolution_add_fusion.5
  292.2 5.1 multiply_reduce_fusion.8
  297.3 57.7 %all-reduce.2 = (f32[]{:T(128)}, f32[]{:T(128)}, f32[]{:T(128)}, f32[]{:T(128)}) all-reduce(f32[]{:T(128)} %get-tuple-element.15, f32[]{:T(128)} %get-tuple-element.13, f32[]{:T(128)} %get-tuple-element.14, f32[]{:T(128)} %get-tuple-element.12), channel_id=1, replica_groups=mesh['seg'=8,'blk'=32] {'blk'}, use_global_device_ids=true, to_apply=%region_13.14 | all-reduce | flops 4 | bytes 32 | tf_op jit(solution)/shard_map/psum | solution.py:90
  360.3 5.6 fusion.115
  365.9 2.7 fusion.19
  369.9 4.8 collective-permute-start.7
  374.7 2.9 fusion.14
  377.5 3.2 convolution_add_fusion.3
  380.8 5.0 multiply_reduce_fusion.4
  385.8 58.1 %all-reduce.1 = (f32[]{:T(128)}, f32[]{:T(128)}, f32[]{:T(128)}, f32[]{:T(128)}) all-reduce(f32[]{:T(128)} %get-tuple-element.11, f32[]{:T(128)} %get-tuple-element.9, f32[]{:T(128)} %get-tuple-element.10, f32[]{:T(128)} %get-tuple-element.8), channel_id=1, replica_groups=mesh['seg'=8,'blk'=32] {'blk'}, use_global_device_ids=true, to_apply=%region_21.22 | all-reduce | flops 4 | bytes 32 | tf_op jit(solution)/shard_map/psum | solution.py:90
  449.1 4.4 fusion.114
  453.5 2.7 fusion.20
  457.4 4.8 collective-permute-start.9
  462.3 2.9 fusion.15
  465.1 3.2 convolution_add_fusion.1
  468.4 4.0 multiply_reduce_fusion
  472.4 57.9 %all-reduce = (f32[]{:T(128)}, f32[]{:T(128)}, f32[]{:T(128)}, f32[]{:T(128)}) all-reduce(f32[]{:T(128)} %get-tuple-element.7, f32[]{:T(128)} %get-tuple-element.5, f32[]{:T(128)} %get-tuple-element.6, f32[]{:T(128)} %get-tuple-element.4), channel_id=1, replica_groups=mesh['seg'=8,'blk'=32] {'blk'}, use_global_device_ids=true, to_apply=%region_29.30 | all-reduce | flops 4 | bytes 32 | tf_op jit(solution)/shard_map/psum | solution.py:90
  535.7 3.5 multiply_bitcast_fusion
  539.2 1.5 fusion.10
  540.7 93.2 %collective-permute-start.11 = (bf16[1,512,512]{2,1,0:T(8,128)(2,1)}, bf16[1,512,512]{2,1,0:T(8,128)(2,1)}, u32[]{:S(2)}, u32[]{:S(2)}) collective-permute-start(bf16[1,512,512]{2,1,0:T(8,128)(2,1)} %fusion.10), channel_id=1, source_target_pairs={{32,0},{64,32},{96,64},{128,96},{160,128},{192,160},{224,192},{33,... | collective-permute-start | bytes 1572872 | tf_op jit(solution)/shard_map/ppermute | solution.py:14
  633.9 1.6 fusion.9
  635.6 3.0 collective-permute-start.10
  638.6 3.6 collective-permute-done.11
  642.2 1.9 fusion.33
  (41 shorter events, 13.3 us)
Async XLA Ops:
  0.6 73.0 %copy-start = (bf16[1,1,512,512]{3,2,1,0:T(8,128)(2,1)S(1)}, bf16[1,1,512,512]{3,2,1,0:T(8,128)(2,1)}, u32[]{:S(2)}) copy-start(bf16[1,1,512,512]{3,2,1,0:T(8,128)(2,1)} %param.11) | copy-start | bytes 1572868
  0.6 0.7 copy-start.6
  0.7 70.5 %copy-start.3 = (bf16[1,1,512,512]{3,2,1,0:T(8,128)(2,1)S(1)}, bf16[1,1,512,512]{3,2,1,0:T(8,128)(2,1)}, u32[]{:S(2)}) copy-start(bf16[1,1,512,512]{3,2,1,0:T(8,128)(2,1)} %param.7) | copy-start | bytes 1572868
  71.2 2.5 copy-start.4
  72.3 8.0 %copy-start.2 = (bf16[1,1,2,512,512]{4,3,2,1,0:T(8,128)(2,1)S(1)}, bf16[1,1,2,512,512]{4,3,2,1,0:T(8,128)(2,1)}, u32[]{:S(2)}) copy-start(bf16[1,1,2,512,512]{4,3,2,1,0:T(8,128)(2,1)} %param.8) | copy-start | bytes 3145732
  72.3 49.6 %collective-permute-start = (bf16[1,512,512]{2,1,0:T(8,128)(2,1)}, bf16[1,512,512]{2,1,0:T(8,128)(2,1)}, u32[]{:S(2)}, u32[]{:S(2)}) collective-permute-start(bf16[1,512,512]{2,1,0:T(8,128)(2,1)} %fusion.113), channel_id=1, source_target_pairs={{1,0},{2,1},{3,2},{4,3},{5,4},{6,5},{7,6},{8,7},{9,8},{10,9},{11,1... | collective-permute-start | bytes 1572872 | tf_op jit(solution)/shard_map/ppermute | solution.py:14
  75.5 46.3 %collective-permute-start.1 = (bf16[1,512,512]{2,1,0:T(8,128)(2,1)}, bf16[1,512,512]{2,1,0:T(8,128)(2,1)}, u32[]{:S(2)}, u32[]{:S(2)}) collective-permute-start(bf16[1,512,512]{2,1,0:T(8,128)(2,1)} %fusion.16), channel_id=1, source_target_pairs={{0,1},{1,2},{2,3},{3,4},{4,5},{5,6},{6,7},{7,8},{8,9},{9,10},{10,1... | collective-permute-start | bytes 1572872 | tf_op jit(solution)/shard_map/ppermute | solution.py:14
  80.3 1.6 copy-start.1
  189.2 12.5 %collective-permute-start.2 = (bf16[1,512,512]{2,1,0:T(8,128)(2,1)}, bf16[1,512,512]{2,1,0:T(8,128)(2,1)}, u32[]{:S(2)}, u32[]{:S(2)}) collective-permute-start(bf16[1,512,512]{2,1,0:T(8,128)(2,1)} %get-tuple-element.48), channel_id=1, source_target_pairs={{1,0},{2,1},{3,2},{4,3},{5,4},{6,5},{7,6},{8,7},{9,8},{10,9},{11,1... | collective-permute-start | bytes 1572872 | tf_op jit(solution)/shard_map/ppermute | solution.py:14
  190.5 11.2 %collective-permute-start.3 = (bf16[1,512,512]{2,1,0:T(8,128)(2,1)}, bf16[1,512,512]{2,1,0:T(8,128)(2,1)}, u32[]{:S(2)}, u32[]{:S(2)}) collective-permute-start(bf16[1,512,512]{2,1,0:T(8,128)(2,1)} %fusion.17), channel_id=1, source_target_pairs={{0,1},{1,2},{2,3},{3,4},{4,5},{5,6},{6,7},{7,8},{8,9},{9,10},{10,1... | collective-permute-start | bytes 1572872 | tf_op jit(solution)/shard_map/ppermute | solution.py:14
  279.9 12.3 %collective-permute-start.4 = (bf16[1,512,512]{2,1,0:T(8,128)(2,1)}, bf16[1,512,512]{2,1,0:T(8,128)(2,1)}, u32[]{:S(2)}, u32[]{:S(2)}) collective-permute-start(bf16[1,512,512]{2,1,0:T(8,128)(2,1)} %get-tuple-element.45), channel_id=1, source_target_pairs={{1,0},{2,1},{3,2},{4,3},{5,4},{6,5},{7,6},{8,7},{9,8},{10,9},{11,1... | collective-permute-start | bytes 1572872 | tf_op jit(solution)/shard_map/ppermute | solution.py:14
  281.1 11.0 %collective-permute-start.5 = (bf16[1,512,512]{2,1,0:T(8,128)(2,1)}, bf16[1,512,512]{2,1,0:T(8,128)(2,1)}, u32[]{:S(2)}, u32[]{:S(2)}) collective-permute-start(bf16[1,512,512]{2,1,0:T(8,128)(2,1)} %fusion.18), channel_id=1, source_target_pairs={{0,1},{1,2},{2,3},{3,4},{4,5},{5,6},{6,7},{7,8},{8,9},{9,10},{10,1... | collective-permute-start | bytes 1572872 | tf_op jit(solution)/shard_map/ppermute | solution.py:14
  288.8 3.3 copy-start.5
  368.6 12.2 %collective-permute-start.6 = (bf16[1,512,512]{2,1,0:T(8,128)(2,1)}, bf16[1,512,512]{2,1,0:T(8,128)(2,1)}, u32[]{:S(2)}, u32[]{:S(2)}) collective-permute-start(bf16[1,512,512]{2,1,0:T(8,128)(2,1)} %get-tuple-element.41), channel_id=1, source_target_pairs={{1,0},{2,1},{3,2},{4,3},{5,4},{6,5},{7,6},{8,7},{9,8},{10,9},{11,1... | collective-permute-start | bytes 1572872 | tf_op jit(solution)/shard_map/ppermute | solution.py:14
  369.9 10.9 %collective-permute-start.7 = (bf16[1,512,512]{2,1,0:T(8,128)(2,1)}, bf16[1,512,512]{2,1,0:T(8,128)(2,1)}, u32[]{:S(2)}, u32[]{:S(2)}) collective-permute-start(bf16[1,512,512]{2,1,0:T(8,128)(2,1)} %fusion.19), channel_id=1, source_target_pairs={{0,1},{1,2},{2,3},{3,4},{4,5},{5,6},{6,7},{7,8},{8,9},{9,10},{10,1... | collective-permute-start | bytes 1572872 | tf_op jit(solution)/shard_map/ppermute | solution.py:14
  456.2 12.2 %collective-permute-start.8 = (bf16[1,512,512]{2,1,0:T(8,128)(2,1)}, bf16[1,512,512]{2,1,0:T(8,128)(2,1)}, u32[]{:S(2)}, u32[]{:S(2)}) collective-permute-start(bf16[1,512,512]{2,1,0:T(8,128)(2,1)} %get-tuple-element.38), channel_id=1, source_target_pairs={{1,0},{2,1},{3,2},{4,3},{5,4},{6,5},{7,6},{8,7},{9,8},{10,9},{11,1... | collective-permute-start | bytes 1572872 | tf_op jit(solution)/shard_map/ppermute | solution.py:14
  457.4 10.9 %collective-permute-start.9 = (bf16[1,512,512]{2,1,0:T(8,128)(2,1)}, bf16[1,512,512]{2,1,0:T(8,128)(2,1)}, u32[]{:S(2)}, u32[]{:S(2)}) collective-permute-start(bf16[1,512,512]{2,1,0:T(8,128)(2,1)} %fusion.20), channel_id=1, source_target_pairs={{0,1},{1,2},{2,3},{3,4},{4,5},{5,6},{6,7},{7,8},{8,9},{9,10},{10,1... | collective-permute-start | bytes 1572872 | tf_op jit(solution)/shard_map/ppermute | solution.py:14
  540.7 101.5 %collective-permute-start.11 = (bf16[1,512,512]{2,1,0:T(8,128)(2,1)}, bf16[1,512,512]{2,1,0:T(8,128)(2,1)}, u32[]{:S(2)}, u32[]{:S(2)}) collective-permute-start(bf16[1,512,512]{2,1,0:T(8,128)(2,1)} %fusion.10), channel_id=1, source_target_pairs={{32,0},{64,32},{96,64},{128,96},{160,128},{192,160},{224,192},{33,... | collective-permute-start | bytes 1572872 | tf_op jit(solution)/shard_map/ppermute | solution.py:14
  635.6 9.4 %collective-permute-start.10 = (bf16[1,512,512]{2,1,0:T(8,128)(2,1)}, bf16[1,512,512]{2,1,0:T(8,128)(2,1)S(1)}, u32[]{:S(2)}, u32[]{:S(2)}) collective-permute-start(bf16[1,512,512]{2,1,0:T(8,128)(2,1)} %fusion.9), channel_id=1, source_target_pairs={{0,32},{32,64},{64,96},{96,128},{128,160},{160,192},{192,224},{1,3... | collective-permute-start | bytes 1572872 | tf_op jit(solution)/shard_map/ppermute | solution.py:14
where the time goes:
time: 658 us; the launch traced here: 647 us
  blocking collectives  354 us (54%)
  starting transfers between devices  127 us (19%)
  matrix products  69.4 us (11%)
  local copies, waits for them, and re-layouts  37 us (6%)
  other arithmetic  28.5 us (4%)
  between operations  26.8 us (4%)
    psum x4, blocking collectives, per_device(): lax.psum((jnp.sum(vector * applied), jnp.sum(correction * applied)), 'blk')  232 us
    ppermute x12, starting transfers between devices, shifted(): return lax.ppermute(block, axis, route)  127 us
    psum x1, blocking collectives, per_device(): norm_total = lax.psum(jnp.sum(vector * vector), 'blk')  65.2 us
    psum x1, blocking collectives, per_device(): energy = lax.psum(jnp.sum(vector * image), 'blk')  56.4 us
    dot_general x10, matrix products, operator(): jnp.einsum('sij,sjk->sik', partial_left, right_factors[:, term_index], pr...  29.6 us
    dot_general x5, matrix products, operator(): jnp.einsum('sij,skj->sik', partial_next, hop_right, preferred_element_typ...  23.7 us
    convert_element_type x5, other arithmetic, operator(): blocks = field.astype(jnp.bfloat16)  18.9 us
    gather x2, local copies, waits for them, and re-layouts, per_device(): jnp.diagonal(right_factors[:, term_index], axis1=1, axis2=2)  16.8 us
  transfers between devices with their start and end apart: 12, of which 2 were waited for; matrix products, arithmetic and copies ran while one was open for 11% of the time, Pallas kernels for 0%

commit v1 on v0

v1 whole, which is shorter than its diff:
```python
import functools
import math

import jax
import jax.numpy as jnp
from jax import lax
from jax.experimental import pallas as pl
from jax.experimental.pallas import tpu as pltpu
from jax.sharding import PartitionSpec as P

ITERS = 4
MESH = pl.DeviceIdType.MESH
F32 = jnp.float32
BF16 = jnp.bfloat16
ROWS = 32
OUTSIDE = 3e38


def dot(a, b):
    return lax.dot_general(a, b, (((1,), (0,)), ((), ())), preferred_element_type=F32)


def dot_nt(a, b):
    return lax.dot_general(a, b, (((1,), (1,)), ((), ())), preferred_element_type=F32)


def fold(x):
    rows, cols = x.shape
    return jnp.sum(x.reshape(rows // 8, 8, cols), axis=0)


def total(x):
    return jnp.sum(jnp.sum(x, axis=0, keepdims=True), axis=1, keepdims=True)


def kernel(
    n, nseg, width,
    guess_h, left_h, right_h, hopl_h, hopr_h, dims, kept,
    ground_o, energy_o, lenv_o, renv_o,
    lv, rv, hl, hlt, hr, gv, diag, vec, img, acc, cb, xr, cs, cr, pp, rm, qq,
    gb, fb, ft, lb, rb, arsrc, arbuf,
    load_sem, xs_sem, xr_sem, cs_sem, cr_sem, as_sem, ar_sem, out_sem, env_s, env_r,
):
    me = lax.axis_index("blk")
    seg = lax.axis_index("seg")
    right, left = lax.rem(me + 1, n), lax.rem(me + n - 1, n)
    half = width // 2
    hs = (pl.ds(0, half), pl.ds(half, half))
    steps = half // ROWS

    loads = [
        pltpu.make_async_copy(src, dst, load_sem.at[i])
        for i, (src, dst) in enumerate(
            ((guess_h, gv), (hopl_h, hl), (hopr_h, hr), (left_h, lv), (right_h, rv))
        )
    ]
    for copy in loads:
        copy.start()
    own_left = pltpu.make_async_copy(left_h.at[0], lenv_o, out_sem.at[1])
    own_right = pltpu.make_async_copy(right_h.at[pl.ds(0, width)], renv_o, out_sem.at[2])

    barrier = pltpu.get_barrier_semaphore()

    def greet(d, _):
        pl.semaphore_signal(
            barrier, inc=1, device_id={"blk": lax.rem(me + d, n)}, device_id_type=MESH
        )
        return 0

    lax.fori_loop(1, n, greet, 0)
    for d in (1, nseg - 1):
        pl.semaphore_signal(
            barrier, inc=1, device_id={"seg": lax.rem(seg + d, nseg)}, device_id_type=MESH
        )

    @pl.when(seg == 0)
    def _():
        own_left.start()

    @pl.when(seg == nseg - 1)
    def _():
        own_right.start()

    live_rows, live_cols = dims[0, 0], dims[0, 1]

    def live(row0, h, rows):
        i = lax.broadcasted_iota(jnp.int32, (rows, half), 0) + row0
        j = lax.broadcasted_iota(jnp.int32, (rows, half), 1) + h * half
        return (i < live_rows) & (j < live_cols)

    def x_copy(par, h, rc):
        rows = pl.ds(rc * half, half)
        return pltpu.make_async_remote_copy(
            src_ref=cb.at[h, rows], dst_ref=xr.at[par, h, rows],
            send_sem=xs_sem.at[h], recv_sem=xr_sem.at[par, h],
            device_id={"blk": left}, device_id_type=MESH,
        )

    def x_whole(par, h):
        return pltpu.make_async_remote_copy(
            src_ref=cb.at[h], dst_ref=xr.at[par, h],
            send_sem=xs_sem.at[h], recv_sem=xr_sem.at[par, h],
            device_id={"blk": left}, device_id_type=MESH,
        )

    def c_copy(par, h):
        return pltpu.make_async_remote_copy(
            src_ref=cs.at[h], dst_ref=cr.at[par, h],
            send_sem=cs_sem.at[h], recv_sem=cr_sem.at[par, h],
            device_id={"blk": right}, device_id_type=MESH,
        )

    loads[0].wait()
    zero_sum = jnp.zeros((8, half), F32)

    def first(h):
        def step(i, weight):
            row0 = pl.multiple_of(i * ROWS, ROWS)
            rows = pl.ds(row0, ROWS)
            c = jnp.where(live(row0, h, ROWS), gv[rows, hs[h]].astype(F32), 0.0)
            cb[h, rows] = c.astype(BF16)
            vec[h, rows] = jnp.zeros((ROWS, half), F32)
            img[h, rows] = jnp.zeros((ROWS, half), F32)
            return weight + fold(c * c)

        return step

    weight0 = zero_sum
    for h in (0, 1):
        weight0 = lax.fori_loop(0, width // ROWS, first(h), weight0)

    pl.semaphore_wait(barrier, n - 1 + 2)
    for h in (0, 1):
        for rc in (0, 1):
            x_copy(0, h, rc).start()

    loads[1].wait()

    @pl.when(me == n - 1)
    def _():
        hl[...] = jnp.zeros_like(hl)

    hlt[...] = hl[...].T
    loads[2].wait()

    def couple(par, halves):
        for h in (0, 1):
            rm[:, hs[h]] = dot(hlt[...], cb[h]).astype(BF16)
        for h in halves:
            cs[h] = dot(rm[...], hr[:, hs[h]]).astype(BF16)
            c_copy(par, h).start()

    def onsite():
        for k in (0, 1):
            for h in (0, 1):
                pp[:, pl.ds(k * width + h * half, half)] = dot(lv[k], cb[h]).astype(BF16)
        for h in (0, 1):
            acc[h] = dot(pp[...], rv[:, hs[h]])

    def ar_whole(par):
        return pltpu.make_async_remote_copy(
            src_ref=arbuf.at[par, pl.ds(0, n - 1)], dst_ref=arbuf.at[par, pl.ds(0, n - 1)],
            send_sem=as_sem.at[par], recv_sem=ar_sem.at[par],
            device_id={"blk": right}, device_id_type=MESH,
        )

    lane = lax.broadcasted_iota(jnp.int32, (1, 128), 1)

    def first_half(par, corr, weight, cross):
        x_whole(par, 0).wait_recv()
        qq[...] = dot(hl[...], xr[par, 0]).astype(BF16)
        c_copy(par, 1).wait_recv()
        curv = jnp.zeros((8, half), F32)
        for h in (0, 1):
            part = dot_nt(qq[...], hr[hs[h], hs[0]])
            local = acc[h]
            terms = local + 2.0 * part
            if h == 1:
                terms = terms + 2.0 * cr[par, 1].astype(F32)
            curv = curv + fold(cb[h].astype(F32) * terms)
            acc[h] = local + part
        sums = [total(s) for s in (corr, weight, cross, curv)]
        row = jnp.zeros((1, 128), F32)
        for k in range(4):
            row = jnp.where(lane == k, sums[k], row)
        arsrc[par, 0:1] = row
        arbuf[par, n - 1 : n] = row
        for d in range(1, n):
            pltpu.make_async_remote_copy(
                src_ref=arsrc.at[par, pl.ds(0, 1)], dst_ref=arbuf.at[par, pl.ds(d - 1, 1)],
                send_sem=as_sem.at[par], recv_sem=ar_sem.at[par],
                device_id={"blk": lax.rem(me + d, n)}, device_id_type=MESH,
            ).start()

    def second_half(par):
        x_whole(par, 1).wait_recv()
        qq[...] = dot(hl[...], xr[par, 1]).astype(BF16)
        for h in (0, 1):
            acc[h] = acc[h] + dot_nt(qq[...], hr[hs[h], hs[1]])
        c_copy(par, 0).wait_recv()

    def coefficients(par, start, energy):
        whole = ar_whole(par)
        whole.wait_recv()
        tot = jnp.sum(arbuf[par], axis=0, keepdims=True)
        corr, weight, cross, curv = (
            jnp.sum(jnp.where(lane == k, tot, 0.0), axis=1, keepdims=True) for k in range(4)
        )
        whole.wait_send()
        span = weight - corr * corr
        length = jnp.sqrt(span)
        off = (cross - corr * energy) / length
        lower = (curv - 2.0 * corr * cross + corr * corr * energy) / span
        gap = (energy - lower) / 2.0
        radius = jnp.sqrt(gap * gap + off * off)
        keep = radius - gap
        turn = -off
        norm = jnp.sqrt(keep * keep + turn * turn)
        scale = turn / (length * norm)
        a = keep / norm - scale * corr
        new = (energy + lower) / 2.0 - radius
        if start is None:
            return a, scale, new
        a = jnp.where(start, 0.0, a)
        scale = jnp.where(start, 1.0 / length, scale)
        new = jnp.where(start, lower, new)
        return a, scale, new

    def sent(halves_x, halves_c):
        for h in halves_x:
            x_whole(0, h).wait_send()
        for h in halves_c:
            c_copy(0, h).wait_send()

    def prepare():
        i = lax.broadcasted_iota(jnp.int32, (128, 128), 0)
        eye = i == lax.broadcasted_iota(jnp.int32, (128, 128), 1)
        for h in (0, 1):
            cols = [
                [
                    jnp.sum(
                        jnp.where(
                            eye,
                            rv[pl.ds(k * width + b, 128), pl.ds(b, 128)].astype(F32),
                            0.0,
                        ),
                        axis=0,
                        keepdims=True,
                    )
                    for b in range(h * half, (h + 1) * half, 128)
                ]
                for k in (0, 1)
            ]
            cols = [jnp.concatenate(c, axis=1) for c in cols]
            for b in range(0, width, 128):
                value = jnp.zeros((128, half), F32)
                for k in (0, 1):
                    block = lv[k, pl.ds(b, 128), pl.ds(b, 128)].astype(F32)
                    col = jnp.sum(jnp.where(eye, block, 0.0), axis=1, keepdims=True)
                    value = value + col * cols[k]
                diag[h, pl.ds(b, 128)] = jnp.where(live(b, h, 128), value, OUTSIDE)

    def update(par, last, a, scale, energy):
        def chunk(q, sums):
            h, rc = q // 2, lax.rem(q, 2)

            def step(i, sums):
                corr, weight, cross = sums
                rows = pl.ds(pl.multiple_of(rc * half + i * ROWS, ROWS), ROWS)
                c = cb[h, rows].astype(F32)
                v = a * vec[h, rows] + scale * c
                m = a * img[h, rows] + scale * (acc[h, rows] + cr[par, h, rows].astype(F32))
                vec[h, rows] = v
                img[h, rows] = m
                d = diag[h, rows]
                w = 1.0 + jnp.abs(d - energy)
                inv = pl.reciprocal(w, approx=True)
                inv = inv * (2.0 - w * inv)
                new = jnp.where(d < OUTSIDE, (m - energy * v) * inv, 0.0).astype(BF16)
                cb[h, rows] = new
                c = new.astype(F32)
                return corr + fold(v * c), weight + fold(c * c), cross + fold(m * c)

            sums = lax.fori_loop(0, steps, step, sums)

            @pl.when(jnp.logical_or(h == 0, jnp.logical_not(last)))
            def _():
                x_copy(1 - par, h, rc).start()

            return sums

        return lax.fori_loop(0, 4, chunk, (zero_sum, zero_sum, zero_sum))

    couple(0, (1, 0))
    loads[3].wait()
    loads[4].wait()
    prepare()

    def iteration(t, carry):
        energy, corr, weight, cross = carry
        par = lax.rem(t, 2)

        @pl.when(t > 0)
        def _():
            couple(par, (1, 0))

        onsite()
        first_half(par, corr, weight, cross)
        second_half(par)
        a, scale, energy = coefficients(par, t == 0, energy)
        sent((0, 1), (0, 1))
        return (energy,) + update(par, t == ITERS - 1, a, scale, energy)

    carry = (jnp.zeros((1, 1), F32), zero_sum, weight0, zero_sum)
    energy, corr, weight, cross = lax.fori_loop(0, ITERS, iteration, carry)
    par = ITERS % 2
    couple(par, (1,))
    onsite()
    first_half(par, corr, weight, cross)
    a, scale, energy = coefficients(par, None, energy)
    energy_o[0] = jnp.sum(energy)

    for h in (0, 1):
        def step(i, _):
            rows = pl.ds(pl.multiple_of(i * ROWS, ROWS), ROWS)
            v = a * vec[h, rows] + scale * cb[h, rows].astype(F32)
            gb[rows, hs[h]] = v * (width * math.sqrt(n))
            fb[rows, hs[h]] = v.astype(BF16)
            return 0

        lax.fori_loop(0, width // ROWS, step, 0)
    ground_copy = pltpu.make_async_copy(gb, ground_o, out_sem.at[0])
    ground_copy.start()

    handoff = n * width * math.sqrt(width)
    size = kept[0, 0]
    i = lax.broadcasted_iota(jnp.int32, (width, half), 0)
    j = lax.broadcasted_iota(jnp.int32, (width, half), 1)

    def kept_part(x, h):
        return jnp.where((i < size) & (j + h * half < size), x * handoff, 0.0).astype(BF16)

    to_next = pltpu.make_async_remote_copy(
        src_ref=lb, dst_ref=lenv_o, send_sem=env_s.at[0], recv_sem=env_r.at[0],
        device_id={"seg": lax.rem(seg + 1, nseg)}, device_id_type=MESH,
    )
    to_previous = pltpu.make_async_remote_copy(
        src_ref=rb, dst_ref=renv_o, send_sem=env_s.at[1], recv_sem=env_r.at[1],
        device_id={"seg": lax.rem(seg + nseg - 1, nseg)}, device_id_type=MESH,
    )
    for h in (0, 1):
        rm[:, hs[h]] = dot(fb[...], rv[pl.ds(0, width), hs[h]]).astype(BF16)
    for h in (0, 1):
        rb[:, hs[h]] = kept_part(dot_nt(rm[...], fb[hs[h], :]), h)

    @pl.when(seg > 0)
    def _():
        to_previous.start()

    ft[...] = fb[...].T
    for h in (0, 1):
        rm[:, hs[h]] = dot(lv[0], fb[:, hs[h]]).astype(BF16)
    for h in (0, 1):
        lb[:, hs[h]] = kept_part(dot(ft[...], rm[:, hs[h]]), h)

    @pl.when(seg < nseg - 1)
    def _():
        to_next.start()

    sent((0,), (1,))
    ground_copy.wait()

    @pl.when(seg > 0)
    def _():
        to_previous.wait_send()
        to_next.wait_recv()

    @pl.when(seg < nseg - 1)
    def _():
        to_next.wait_send()
        to_previous.wait_recv()

    @pl.when(seg == 0)
    def _():
        own_left.wait()

    @pl.when(seg == nseg - 1)
    def _():
        own_right.wait()


def per_device(
    guess_blocks, onsite_left, onsite_right, hopping_left, hopping_right, sector_dims, kept_dims
):
    n, nseg = lax.axis_size("blk"), lax.axis_size("seg")
    width = guess_blocks.shape[-1]
    half = width // 2
    square, halves = (width, width), (2, width, half)
    hbm = pl.BlockSpec(memory_space=pltpu.HBM)
    smem = pl.BlockSpec(memory_space=pltpu.SMEM)
    dma = pltpu.SemaphoreType.DMA
    scratch = [
        pltpu.VMEM((2,) + square, BF16),
        pltpu.VMEM((2 * width, width), BF16),
        pltpu.VMEM(square, BF16),
        pltpu.VMEM(square, BF16),
        pltpu.VMEM(square, BF16),
        pltpu.VMEM(square, BF16),
        pltpu.VMEM(halves, F32),
        pltpu.VMEM(halves, F32),
        pltpu.VMEM(halves, F32),
        pltpu.VMEM(halves, F32),
        pltpu.VMEM(halves, BF16),
        pltpu.VMEM((2,) + halves, BF16),
        pltpu.VMEM(halves, BF16),
        pltpu.VMEM((2,) + halves, BF16),
        pltpu.VMEM((width, 2 * width), BF16),
        pltpu.VMEM(square, BF16),
        pltpu.VMEM((width, half), BF16),
        pltpu.VMEM(square, F32),
        pltpu.VMEM(square, BF16),
        pltpu.VMEM(square, BF16),
        pltpu.VMEM(square, BF16),
        pltpu.VMEM(square, BF16),
        pltpu.VMEM((2, 8, 128), F32),
        pltpu.VMEM((2, n, 128), F32),
        dma((5,)), dma((2,)), dma((2, 2)), dma((2,)), dma((2, 2)), dma((2,)), dma((2,)),
        dma((3,)), dma((2,)), dma((2,)),
    ]
    ground, energy, lenv, renv = pl.pallas_call(
        functools.partial(kernel, n, nseg, width),
        out_shape=(
            jax.ShapeDtypeStruct(square, F32),
            jax.ShapeDtypeStruct((1,), F32),
            jax.ShapeDtypeStruct(square, BF16),
            jax.ShapeDtypeStruct(square, BF16),
        ),
        in_specs=[hbm] * 5 + [smem] * 2,
        out_specs=(hbm, smem, hbm, hbm),
        scratch_shapes=scratch,
        compiler_params=pltpu.CompilerParams(
            collective_id=0, has_side_effects=True, vmem_limit_bytes=60 * 2**20
        ),
    )(
        guess_blocks[0, 0],
        onsite_left[0, 0],
        onsite_right[0, 0].reshape(2 * width, width),
        hopping_left[0, 0],
        hopping_right[0, 0],
        sector_dims[0],
        kept_dims,
    )
    return ground[None, None], energy, lenv[None, None], renv[None, None]


def solution(mesh):
    in_specs = (
        P("seg", "blk", None, None),
        P("seg", "blk", None, None, None),
        P("seg", "blk", None, None, None),
        P("seg", "blk", None, None),
        P("seg", "blk", None, None),
        P("seg", "blk", None),
        P("seg", "blk"),
    )
    out_specs = (
        P("seg", "blk", None, None),
        P("seg"),
        P("seg", "blk", None, None),
        P("seg", "blk", None, None),
    )
    return jax.shard_map(
        per_device, mesh=mesh, in_specs=in_specs, out_specs=out_specs, check_vma=False
    )
```

time: 658 us -> 108 us (0.16); the launches traced: 647 us -> 108 us
  blocking collectives: 354 us -> 0 us
  starting transfers between devices: 127 us -> 0 us
  Pallas kernels: 0 us -> 100 us
  matrix products: 69.4 us -> 0 us
  local copies, waits for them, and re-layouts: 37 us -> 4.34 us
  other arithmetic: 28.5 us -> 0 us
  between operations: 26.8 us -> 2.99 us
    psum x6 -> x0, blocking collectives: 354 us -> none  [the longest x4 232 us: per_device(): lax.psum((jnp.sum(vector * applied), jnp.sum(correction * applied)), 'blk')]
    ppermute x12 -> x0, starting transfers between devices: 127 us -> none  [shifted(): return lax.ppermute(block, axis, route)]
    pallas_call x0 -> x1, Pallas kernels: none -> 100 us  [per_device(): pl.pallas_call(functools.partial(kernel, n, nseg, width), out_shape=(jax....]
    dot_general x22 -> x0, matrix products: 69.4 us -> none  [the longest x10 29.6 us: operator(): jnp.einsum('sij,sjk->sik', partial_left, right_factors[:, term_index], pr...]
    gather x4 -> x0, local copies, waits for them, and re-layouts: 33 us -> none  [the longest x2 16.8 us: per_device(): jnp.diagonal(right_factors[:, term_index], axis1=1, axis2=2)]
    convert_element_type x9 -> x0, other arithmetic: 18.9 us -> none  [the longest x5 18.9 us: operator(): blocks = field.astype(jnp.bfloat16)]
  transfers between devices with their start and end apart: 12 -> 0, of which waited for: 2 -> 0; matrix products, arithmetic and copies ran while one was open for 11% -> 0% of each run, Pallas kernels for 0% -> 0%
where the time goes in v1:
time: 108 us
  Pallas kernels  100 us (93%)
  local copies, waits for them, and re-layouts  4.34 us (4%)
  between operations  2.99 us (3%)
    pallas_call x1, Pallas kernels, per_device(): pl.pallas_call(functools.partial(kernel, n, nseg, width), out_shape=(jax....  100 us
    unnamed x7, local copies, waits for them, and re-layouts  4.34 us

profile of v1, /device:TPU:1, one launch (start us, length us, event | category | flops | bytes accessed | tf_op | source)
XLA Modules:
  0.0 107.8 jit_solution(8588800136876488334)
XLA Ops:
  1.3 100.5 %shard_map.102 = (f32[512,512]{1,0:T(8,128)}, f32[1]{0:T(128)}, bf16[512,512]{1,0:T(8,128)(2,1)}, bf16[512,512]{1,0:T(8,128)(2,1)}) custom-call(bf16[512,512]{1,0:T(8,128)(2,1)} %bitcast.14, bf16[2,512,512]{2,1,0:T(8,128)(2,1)} %bitcast.10, bf16[1024,512]{1,0:T(8,128)(2,1)} %bitcast.11, bf16[512,512]{1,0:T(8,128)(2,1)} %bitcast.15, ...), custom_call_target="tpu_custom_call" | custom-call | tf_op jit(solution)/shard_map/pallas_call | solution.py:430
  101.7 0.0 copy-start.1
  101.8 2.3 %copy.16 = f32[1,1,512,512]{3,2,1,0:T(8,128)} copy(f32[1,1,512,512]{3,2,1,0:T(8,128)} %bitcast.9) | data formatting | bytes 2097152
  104.6 0.0 copy-done.1
  104.6 0.0 copy-start
  104.6 0.8 copy.18
  105.4 0.4 copy-done
  105.9 0.8 copy.19
Async XLA Ops:
  101.7 2.9 %copy-start.1 = (bf16[512,512]{1,0:T(8,128)(2,1)S(1)}, bf16[512,512]{1,0:T(8,128)(2,1)}, u32[]{:S(2)}) copy-start(bf16[512,512]{1,0:T(8,128)(2,1)} %get-tuple-element.10) | copy-start | bytes 1572868
  104.6 1.2 %copy-start = (bf16[512,512]{1,0:T(8,128)(2,1)S(1)}, bf16[512,512]{1,0:T(8,128)(2,1)}, u32[]{:S(2)}) copy-start(bf16[512,512]{1,0:T(8,128)(2,1)} %get-tuple-element.11) | copy-start | bytes 1572868

commit v2 on v1

--- a/solution.py
+++ b/solution.py
@@ -35,11 +35,12 @@
 
 def kernel(
     n, nseg, width,
-    guess_h, left_h, right_h, hopl_h, hopr_h, dims, kept,
+    guess_h, left_h, right_h, hopl_h, hopr_h, dims_h, kept_h,
     ground_o, energy_o, lenv_o, renv_o,
-    lv, rv, hl, hlt, hr, gv, diag, vec, img, acc, cb, xr, cs, cr, pp, rm, qq,
-    gb, fb, ft, lb, rb, arsrc, arbuf,
+    lv, rv, hl, hlt, hrc, gv, diag, vec, img, acc, cb, xr, cs, cr, pp, rm, qq,
+    ff, tt, xx, yy, lsend, rsend, lrecv, rrecv, ratio, ratio_in, arsrc, arbuf, dims, kept,
     load_sem, xs_sem, xr_sem, cs_sem, cr_sem, as_sem, ar_sem, out_sem, env_s, env_r,
+    ratio_s, ratio_r,
 ):
     me = lax.axis_index("blk")
     seg = lax.axis_index("seg")
@@ -51,7 +52,16 @@
     loads = [
         pltpu.make_async_copy(src, dst, load_sem.at[i])
         for i, (src, dst) in enumerate(
-            ((guess_h, gv), (hopl_h, hl), (hopr_h, hr), (left_h, lv), (right_h, rv))
+            (
+                (dims_h, dims),
+                (guess_h, gv),
+                (hopl_h, hl),
+                (hopr_h.at[:, hs[0]], hrc.at[0]),
+                (hopr_h.at[:, hs[1]], hrc.at[1]),
+                (left_h, lv),
+                (right_h, rv),
+                (kept_h, kept),
+            )
         )
     ]
     for copy in loads:
@@ -81,6 +91,7 @@
     def _():
         own_right.start()
 
+    loads[0].wait()
     live_rows, live_cols = dims[0, 0], dims[0, 1]
 
     def live(row0, h, rows):
@@ -110,7 +121,7 @@
             device_id={"blk": right}, device_id_type=MESH,
         )
 
-    loads[0].wait()
+    loads[1].wait()
     zero_sum = jnp.zeros((8, half), F32)
 
     def first(h):
@@ -119,8 +130,6 @@
             rows = pl.ds(row0, ROWS)
             c = jnp.where(live(row0, h, ROWS), gv[rows, hs[h]].astype(F32), 0.0)
             cb[h, rows] = c.astype(BF16)
-            vec[h, rows] = jnp.zeros((ROWS, half), F32)
-            img[h, rows] = jnp.zeros((ROWS, half), F32)
             return weight + fold(c * c)
 
         return step
@@ -134,20 +143,21 @@
         for rc in (0, 1):
             x_copy(0, h, rc).start()
 
-    loads[1].wait()
+    loads[2].wait()
 
     @pl.when(me == n - 1)
     def _():
         hl[...] = jnp.zeros_like(hl)
 
     hlt[...] = hl[...].T
-    loads[2].wait()
+    loads[3].wait()
+    loads[4].wait()
 
     def couple(par, halves):
         for h in (0, 1):
             rm[:, hs[h]] = dot(hlt[...], cb[h]).astype(BF16)
         for h in halves:
-            cs[h] = dot(rm[...], hr[:, hs[h]]).astype(BF16)
+            cs[h] = dot(rm[...], hrc[h]).astype(BF16)
             c_copy(par, h).start()
 
     def onsite():
@@ -166,17 +176,17 @@
 
     lane = lax.broadcasted_iota(jnp.int32, (1, 128), 1)
 
-    def first_half(par, corr, weight, cross):
-        x_whole(par, 0).wait_recv()
-        qq[...] = dot(hl[...], xr[par, 0]).astype(BF16)
-        c_copy(par, 1).wait_recv()
+    def first_half(par, f, corr, weight, cross):
+        x_whole(par, f).wait_recv()
+        qq[...] = dot(hl[...], xr[par, f]).astype(BF16)
+        c_copy(par, 1 - f).wait_recv()
         curv = jnp.zeros((8, half), F32)
-        for h in (0, 1):
-            part = dot_nt(qq[...], hr[hs[h], hs[0]])
+        for h in (f, 1 - f):
+            part = dot_nt(qq[...], hrc[f, pl.ds(h * half, half)])
             local = acc[h]
             terms = local + 2.0 * part
-            if h == 1:
-                terms = terms + 2.0 * cr[par, 1].astype(F32)
+            if h is not f:
+                terms = terms + 2.0 * cr[par, h].astype(F32)
             curv = curv + fold(cb[h].astype(F32) * terms)
             acc[h] = local + part
         sums = [total(s) for s in (corr, weight, cross, curv)]
@@ -192,12 +202,11 @@
                 device_id={"blk": lax.rem(me + d, n)}, device_id_type=MESH,
             ).start()
 
-    def second_half(par):
-        x_whole(par, 1).wait_recv()
-        qq[...] = dot(hl[...], xr[par, 1]).astype(BF16)
+    def second_half(par, f):
+        x_whole(par, 1 - f).wait_recv()
+        qq[...] = dot(hl[...], xr[par, 1 - f]).astype(BF16)
         for h in (0, 1):
-            acc[h] = acc[h] + dot_nt(qq[...], hr[hs[h], hs[1]])
-        c_copy(par, 0).wait_recv()
+            acc[h] = acc[h] + dot_nt(qq[...], hrc[1 - f, hs[h]])
 
     def coefficients(par, start, energy):
         whole = ar_whole(par)
@@ -226,13 +235,9 @@
         new = jnp.where(start, lower, new)
         return a, scale, new
 
-    def sent(halves_x, halves_c):
-        for h in halves_x:
-            x_whole(0, h).wait_send()
-        for h in halves_c:
-            c_copy(0, h).wait_send()
-
     def prepare():
+        vec[...] = jnp.zeros_like(vec)
+        img[...] = jnp.zeros_like(img)
         i = lax.broadcasted_iota(jnp.int32, (128, 128), 0)
         eye = i == lax.broadcasted_iota(jnp.int32, (128, 128), 1)
         for h in (0, 1):
@@ -260,125 +265,187 @@
                     value = value + col * cols[k]
                 diag[h, pl.ds(b, 128)] = jnp.where(live(b, h, 128), value, OUTSIDE)
 
-    def update(par, last, a, scale, energy):
-        def chunk(q, sums):
-            h, rc = q // 2, lax.rem(q, 2)
-
-            def step(i, sums):
-                corr, weight, cross = sums
-                rows = pl.ds(pl.multiple_of(rc * half + i * ROWS, ROWS), ROWS)
-                c = cb[h, rows].astype(F32)
-                v = a * vec[h, rows] + scale * c
-                m = a * img[h, rows] + scale * (acc[h, rows] + cr[par, h, rows].astype(F32))
-                vec[h, rows] = v
-                img[h, rows] = m
-                d = diag[h, rows]
-                w = 1.0 + jnp.abs(d - energy)
-                inv = pl.reciprocal(w, approx=True)
-                inv = inv * (2.0 - w * inv)
-                new = jnp.where(d < OUTSIDE, (m - energy * v) * inv, 0.0).astype(BF16)
-                cb[h, rows] = new
-                c = new.astype(F32)
-                return corr + fold(v * c), weight + fold(c * c), cross + fold(m * c)
-
-            sums = lax.fori_loop(0, steps, step, sums)
-
-            @pl.when(jnp.logical_or(h == 0, jnp.logical_not(last)))
-            def _():
-                x_copy(1 - par, h, rc).start()
-
-            return sums
-
-        return lax.fori_loop(0, 4, chunk, (zero_sum, zero_sum, zero_sum))
+    def update(par, f, last, a, scale, energy):
+        sums = (zero_sum, zero_sum, zero_sum)
+        for h in (1 - f, f):
+            if h is f:
+                c_copy(par, f).wait_recv()
+
+            def chunk(rc, sums, h=h):
+                def step(i, sums):
+                    corr, weight, cross = sums
+                    rows = pl.ds(pl.multiple_of(rc * half + i * ROWS, ROWS), ROWS)
+                    c = cb[h, rows].astype(F32)
+                    v = a * vec[h, rows] + scale * c
+                    m = a * img[h, rows] + scale * (acc[h, rows] + cr[par, h, rows].astype(F32))
+                    vec[h, rows] = v
+                    img[h, rows] = m
+                    d = diag[h, rows]
+                    w = 1.0 + jnp.abs(d - energy)
+                    inv = pl.reciprocal(w, approx=True)
+                    inv = inv * (2.0 - w * inv)
+                    new = jnp.where(d < OUTSIDE, (m - energy * v) * inv, 0.0).astype(BF16)
+                    cb[h, rows] = new
+                    c = new.astype(F32)
+                    return corr + fold(v * c), weight + fold(c * c), cross + fold(m * c)
+
+                sums = lax.fori_loop(0, steps, step, sums)
+                if h is not f:
+                    x_copy(1 - par, h, rc).start()
+                else:
+
+                    @pl.when(jnp.logical_not(last))
+                    def _():
+                        x_copy(1 - par, h, rc).start()
+
+                return sums
+
+            sums = lax.fori_loop(0, 2, chunk, sums)
+        return sums
 
     couple(0, (1, 0))
-    loads[3].wait()
-    loads[4].wait()
+    loads[5].wait()
+    loads[6].wait()
     prepare()
 
     def iteration(t, carry):
         energy, corr, weight, cross = carry
         par = lax.rem(t, 2)
+        f = par
 
         @pl.when(t > 0)
         def _():
-            couple(par, (1, 0))
+            for h in (0, 1):
+                c_copy(0, h).wait_send()
+            couple(par, (1 - f, f))
 
         onsite()
-        first_half(par, corr, weight, cross)
-        second_half(par)
+        first_half(par, f, corr, weight, cross)
+        second_half(par, f)
         a, scale, energy = coefficients(par, t == 0, energy)
-        sent((0, 1), (0, 1))
-        return (energy,) + update(par, t == ITERS - 1, a, scale, energy)
+        for h in (0, 1):
+            x_whole(0, h).wait_send()
+        return (energy,) + update(par, f, t == ITERS - 1, a, scale, energy)
 
     carry = (jnp.zeros((1, 1), F32), zero_sum, weight0, zero_sum)
     energy, corr, weight, cross = lax.fori_loop(0, ITERS, iteration, carry)
     par = ITERS % 2
-    couple(par, (1,))
+    f = par
+    for h in (0, 1):
+        c_copy(0, h).wait_send()
+    couple(par, (1 - f,))
     onsite()
-    first_half(par, corr, weight, cross)
+
+    loads[7].wait()
+    size = kept[0, 0]
+    quarters = ((0, 0), (1, 0), (1, 1))
+
+    def env_copy(which, part):
+        src, dst = ((lsend, lrecv), (rsend, rrecv))[which]
+        other = lax.rem(seg + (1, nseg - 1)[which], nseg)
+        if part is not None:
+            src, dst = src.at[part], dst.at[part]
+        return pltpu.make_async_remote_copy(
+            src_ref=src, dst_ref=dst, send_sem=env_s.at[which], recv_sem=env_r.at[which],
+            device_id={"seg": other}, device_id_type=MESH,
+        )
+
+    def ratio_copy(which):
+        other = lax.rem(seg + (1, nseg - 1)[which], nseg)
+        return pltpu.make_async_remote_copy(
+            src_ref=ratio.at[pl.ds(0, 1)], dst_ref=ratio_in.at[which, pl.ds(0, 1)],
+            send_sem=ratio_s.at[which], recv_sem=ratio_r.at[which],
+            device_id={"seg": other}, device_id_type=MESH,
+        )
+
+    sends = (seg < nseg - 1, seg > 0)
+    i = lax.broadcasted_iota(jnp.int32, (half, half), 0)
+    j = lax.broadcasted_iota(jnp.int32, (half, half), 1)
+    first, second = pl.ds(0, width), pl.ds(width, width)
+    for h in (0, 1):
+        ff[:, hs[h]] = cb[h]
+        ff[:, pl.ds(width + h * half, half)] = vec[h].astype(BF16)
+    tt[:, first] = ff[:, first].T
+    tt[:, second] = ff[:, second].T
+    for h in (0, 1):
+        xx[first, hs[h]] = dot(lv[0], ff[:, pl.ds(width + h * half, half)]).astype(BF16)
+        yy[:, hs[h]] = dot(ff[:, second], rv[first, hs[h]]).astype(BF16)
+    xx[second, :] = pp[:, first]
+    for h in (0, 1):
+        yy[:, pl.ds(width + h * half, half)] = dot(ff[:, first], rv[first, hs[h]]).astype(BF16)
+    everything = pl.ds(0, 2 * width)
+    for part, (ours, theirs) in enumerate(
+        ((second, first), (everything, everything), (first, second))
+    ):
+        for q, (r, h) in enumerate(quarters):
+            mask = (i + r * half < size) & (j + h * half < size)
+            x = dot(tt[hs[r], ours], xx[theirs, hs[h]])
+            lsend[part, q] = jnp.where(mask, x, 0.0).astype(BF16)
+
+        @pl.when(sends[0])
+        def _():
+            env_copy(0, part).start()
+
+        for q, (r, h) in enumerate(quarters):
+            mask = (i + r * half < size) & (j + h * half < size)
+            x = dot_nt(yy[hs[r], theirs], ff[hs[h], ours])
+            rsend[part, q] = jnp.where(mask, x, 0.0).astype(BF16)
+
+        @pl.when(sends[1])
+        def _():
+            env_copy(1, part).start()
+
+    first_half(par, f, corr, weight, cross)
     a, scale, energy = coefficients(par, None, energy)
-    energy_o[0] = jnp.sum(energy)
-
-    for h in (0, 1):
+    ratio[...] = jnp.broadcast_to(jnp.where(lane == 0, a, scale), (8, 128))
+    for which in (0, 1):
+
+        @pl.when(sends[which])
+        def _():
+            ratio_copy(which).start()
+
+    energy_o[...] = jnp.broadcast_to(energy, (8, 128))
+    for h in (0, 1):
+
         def step(i, _):
             rows = pl.ds(pl.multiple_of(i * ROWS, ROWS), ROWS)
             v = a * vec[h, rows] + scale * cb[h, rows].astype(F32)
-            gb[rows, hs[h]] = v * (width * math.sqrt(n))
-            fb[rows, hs[h]] = v.astype(BF16)
+            ground_o[rows, hs[h]] = v * (width * math.sqrt(n))
             return 0
 
         lax.fori_loop(0, width // ROWS, step, 0)
-    ground_copy = pltpu.make_async_copy(gb, ground_o, out_sem.at[0])
-    ground_copy.start()
 
     handoff = n * width * math.sqrt(width)
-    size = kept[0, 0]
-    i = lax.broadcasted_iota(jnp.int32, (width, half), 0)
-    j = lax.broadcasted_iota(jnp.int32, (width, half), 1)
-
-    def kept_part(x, h):
-        return jnp.where((i < size) & (j + h * half < size), x * handoff, 0.0).astype(BF16)
-
-    to_next = pltpu.make_async_remote_copy(
-        src_ref=lb, dst_ref=lenv_o, send_sem=env_s.at[0], recv_sem=env_r.at[0],
-        device_id={"seg": lax.rem(seg + 1, nseg)}, device_id_type=MESH,
-    )
-    to_previous = pltpu.make_async_remote_copy(
-        src_ref=rb, dst_ref=renv_o, send_sem=env_s.at[1], recv_sem=env_r.at[1],
-        device_id={"seg": lax.rem(seg + nseg - 1, nseg)}, device_id_type=MESH,
-    )
-    for h in (0, 1):
-        rm[:, hs[h]] = dot(fb[...], rv[pl.ds(0, width), hs[h]]).astype(BF16)
-    for h in (0, 1):
-        rb[:, hs[h]] = kept_part(dot_nt(rm[...], fb[hs[h], :]), h)
+
+    def combine(which, got, out):
+        env_copy(which, None).wait_recv()
+        ratio_copy(which).wait_recv()
+        row = ratio_in[which, 0:1]
+        a = jnp.sum(jnp.where(lane == 0, row, 0.0), axis=1, keepdims=True)
+        b = jnp.sum(jnp.where(lane == 1, row, 0.0), axis=1, keepdims=True)
+        weights = (handoff * a * a, handoff * a * b, handoff * b * b)
+        for q, (r, h) in enumerate(quarters):
+            x = sum(weights[part] * got[part, q].astype(F32) for part in range(3))
+            out[hs[r], hs[h]] = x.astype(BF16)
+            if r != h:
+                out[hs[h], hs[r]] = x.T.astype(BF16)
 
     @pl.when(seg > 0)
     def _():
-        to_previous.start()
-
-    ft[...] = fb[...].T
-    for h in (0, 1):
-        rm[:, hs[h]] = dot(lv[0], fb[:, hs[h]]).astype(BF16)
-    for h in (0, 1):
-        lb[:, hs[h]] = kept_part(dot(ft[...], rm[:, hs[h]]), h)
+        combine(0, lrecv, lenv_o)
 
     @pl.when(seg < nseg - 1)
     def _():
-        to_next.start()
-
-    sent((0,), (1,))
-    ground_copy.wait()
-
-    @pl.when(seg > 0)
-    def _():
-        to_previous.wait_send()
-        to_next.wait_recv()
-
-    @pl.when(seg < nseg - 1)
-    def _():
-        to_next.wait_send()
-        to_previous.wait_recv()
+        combine(1, rrecv, renv_o)
+
+    x_whole(0, f).wait_send()
+    c_copy(0, 1 - f).wait_send()
+    for which in (0, 1):
+
+        @pl.when(sends[which])
+        def _():
+            env_copy(which, None).wait_send()
+            ratio_copy(which).wait_send()
 
     @pl.when(seg == 0)
     def _():
@@ -387,6 +454,18 @@
     @pl.when(seg == nseg - 1)
     def _():
         own_right.wait()
+
+
+def store(ground, energy, lenv, renv, ground_o, energy_o, lenv_o, renv_o, sem):
+    copies = [
+        pltpu.make_async_copy(src, dst.at[0, 0], sem.at[i])
+        for i, (src, dst) in enumerate(((ground, ground_o), (lenv, lenv_o), (renv, renv_o)))
+    ]
+    for copy in copies:
+        copy.start()
+    energy_o[0] = energy[0, 0]
+    for copy in copies:
+        copy.wait()
 
 
 def per_device(
@@ -396,7 +475,10 @@
     width = guess_blocks.shape[-1]
     half = width // 2
     square, halves = (width, width), (2, width, half)
+    forms = (3, 3, half, half)
     hbm = pl.BlockSpec(memory_space=pltpu.HBM)
+    vmem = pl.BlockSpec(memory_space=pltpu.VMEM)
+    any_space = pl.BlockSpec(memory_space=pl.ANY)
     smem = pl.BlockSpec(memory_space=pltpu.SMEM)
     dma = pltpu.SemaphoreType.DMA
     scratch = [
@@ -404,7 +486,7 @@
         pltpu.VMEM((2 * width, width), BF16),
         pltpu.VMEM(square, BF16),
         pltpu.VMEM(square, BF16),
-        pltpu.VMEM(square, BF16),
+        pltpu.VMEM(halves, BF16),
         pltpu.VMEM(square, BF16),
         pltpu.VMEM(halves, F32),
         pltpu.VMEM(halves, F32),
@@ -417,29 +499,36 @@
         pltpu.VMEM((width, 2 * width), BF16),
         pltpu.VMEM(square, BF16),
         pltpu.VMEM((width, half), BF16),
-        pltpu.VMEM(square, F32),
-        pltpu.VMEM(square, BF16),
-        pltpu.VMEM(square, BF16),
-        pltpu.VMEM(square, BF16),
-        pltpu.VMEM(square, BF16),
+        pltpu.VMEM((width, 2 * width), BF16),
+        pltpu.VMEM((width, 2 * width), BF16),
+        pltpu.VMEM((2 * width, width), BF16),
+        pltpu.VMEM((width, 2 * width), BF16),
+        pltpu.VMEM(forms, BF16),
+        pltpu.VMEM(forms, BF16),
+        pltpu.VMEM(forms, BF16),
+        pltpu.VMEM(forms, BF16),
+        pltpu.VMEM((8, 128), F32),
+        pltpu.VMEM((2, 8, 128), F32),
         pltpu.VMEM((2, 8, 128), F32),
         pltpu.VMEM((2, n, 128), F32),
-        dma((5,)), dma((2,)), dma((2, 2)), dma((2,)), dma((2, 2)), dma((2,)), dma((2,)),
-        dma((3,)), dma((2,)), dma((2,)),
+        pltpu.SMEM((1, 2), jnp.int32),
+        pltpu.SMEM((1, 1), jnp.int32),
+        dma((8,)), dma((2,)), dma((2, 2)), dma((2,)), dma((2, 2)), dma((2,)), dma((2,)),
+        dma((3,)), dma((2,)), dma((2,)), dma((2,)), dma((2,)),
     ]
-    ground, energy, lenv, renv = pl.pallas_call(
+    results = pl.pallas_call(
         functools.partial(kernel, n, nseg, width),
         out_shape=(
-            jax.ShapeDtypeStruct(square, F32),
-            jax.ShapeDtypeStruct((1,), F32),
-            jax.ShapeDtypeStruct(square, BF16),
-            jax.ShapeDtypeStruct(square, BF16),
+            pltpu.VMEM(square, F32),
+            pltpu.VMEM((8, 128), F32),
+            pltpu.VMEM(square, BF16),
+            pltpu.VMEM(square, BF16),
         ),
-        in_specs=[hbm] * 5 + [smem] * 2,
-        out_specs=(hbm, smem, hbm, hbm),
+        in_specs=[hbm] * 7,
+        out_specs=(vmem,) * 4,
         scratch_shapes=scratch,
         compiler_params=pltpu.CompilerParams(
-            collective_id=0, has_side_effects=True, vmem_limit_bytes=60 * 2**20
+            collective_id=0, has_side_effects=True, vmem_limit_bytes=58 * 2**20
         ),
     )(
         guess_blocks[0, 0],
@@ -450,7 +539,19 @@
         sector_dims[0],
         kept_dims,
     )
-    return ground[None, None], energy, lenv[None, None], renv[None, None]
+    return pl.pallas_call(
+        store,
+        out_shape=(
+            jax.ShapeDtypeStruct((1, 1) + square, F32),
+            jax.ShapeDtypeStruct((1,), F32),
+            jax.ShapeDtypeStruct((1, 1) + square, BF16),
+            jax.ShapeDtypeStruct((1, 1) + square, BF16),
+        ),
+        in_specs=[vmem] * 4,
+        out_specs=(any_space, smem, any_space, any_space),
+        scratch_shapes=[dma((3,))],
+        compiler_params=pltpu.CompilerParams(vmem_limit_bytes=2**20),
+    )(*results)
 
 
 def solution(mesh):

time: 108 us -> 98.8 us (0.915)
  local copies, waits for them, and re-layouts: 4.34 us -> 0 us
  Pallas kernels: 100 us -> 97.4 us
  between operations: 2.99 us -> 1.29 us
    unnamed x7 -> x0, local copies, waits for them, and re-layouts: 4.34 us -> none
    pallas_call x1 -> x2, Pallas kernels: 100 us -> 97.4 us  [the longest x1 95.6 us: per_device(): pl.pallas_call(functools.partial(kernel, n, nseg, width), out_shape=(pltp...]
where the time goes in v2:
time: 98.8 us; the launch traced here: 98.7 us
  Pallas kernels  97.4 us (99%)
  between operations  1.29 us (1%)
    pallas_call x1, Pallas kernels, per_device(): pl.pallas_call(functools.partial(kernel, n, nseg, width), out_shape=(pltp...  95.6 us

profile of v2, /device:TPU:1, one launch (start us, length us, event | category | flops | bytes accessed | tf_op | source)
XLA Modules:
  0.0 98.7 jit_solution(17545306727616989617)
XLA Ops:
  1.3 95.6 %shard_map.102 = (f32[512,512]{1,0:T(8,128)S(1)}, f32[8,128]{1,0:T(8,128)S(1)}, bf16[512,512]{1,0:T(8,128)(2,1)S(1)}, bf16[512,512]{1,0:T(8,128)(2,1)S(1)}) custom-call(bf16[512,512]{1,0:T(8,128)(2,1)} %bitcast.8, bf16[2,512,512]{2,1,0:T(8,128)(2,1)} %bitcast.6, bf16[1024,512]{1,0:T(8,128)(2,1)} %bitcast.7, bf16[512,512]{1,0:T(8,128)(2,1)} %bitcast.9, ...), custom_call_target="tpu_custom_call" | custom-call | tf_op jit(solution)/shard_map/pallas_call | solution.py:519
  96.9 1.9 %shard_map.103 = (f32[1,1,512,512]{3,2,1,0:T(8,128)}, f32[1]{0:T(128)}, bf16[1,1,512,512]{3,2,1,0:T(8,128)(2,1)}, bf16[1,1,512,512]{3,2,1,0:T(8,128)(2,1)}) custom-call(f32[512,512]{1,0:T(8,128)S(1)} %get-tuple-element.8.ground, f32[8,128]{1,0:T(8,128)S(1)} %get-tuple-element.9.energy, bf16[512,512]{1,0:T(8,128)(2,1)S(1)} %get-tuple-element.10.lenv, ...), custom_call_target="tpu_custom_call" | custom-call | tf_op jit(solution)/shard_map/pallas_call | solution.py:542

commit v3 on v2

--- a/solution.py
+++ b/solution.py
@@ -12,6 +12,7 @@
 MESH = pl.DeviceIdType.MESH
 F32 = jnp.float32
 BF16 = jnp.bfloat16
+SIDE = 4
 ROWS = 32
 OUTSIDE = 3e38
 
@@ -36,11 +37,11 @@
 def kernel(
     n, nseg, width,
     guess_h, left_h, right_h, hopl_h, hopr_h, dims_h, kept_h,
-    ground_o, energy_o, lenv_o, renv_o,
+    ground_o, energy_o, lrecv, rrecv, ratio_in,
     lv, rv, hl, hlt, hrc, gv, diag, vec, img, acc, cb, xr, cs, cr, pp, rm, qq,
-    ff, tt, xx, yy, lsend, rsend, lrecv, rrecv, ratio, ratio_in, arsrc, arbuf, dims, kept,
-    load_sem, xs_sem, xr_sem, cs_sem, cr_sem, as_sem, ar_sem, out_sem, env_s, env_r,
-    ratio_s, ratio_r,
+    ff, tt, xx, yy, lsend, rsend, ratio, arsrc, arbuf, dims, kept,
+    load_sem, xs_sem, xr_sem, cs_sem, cr_sem, as_sem, ar_sem, env_s, env_r,
+    ratio_s, ratio_r, ready,
 ):
     me = lax.axis_index("blk")
     seg = lax.axis_index("seg")
@@ -66,30 +67,41 @@
     ]
     for copy in loads:
         copy.start()
-    own_left = pltpu.make_async_copy(left_h.at[0], lenv_o, out_sem.at[1])
-    own_right = pltpu.make_async_copy(right_h.at[pl.ds(0, width)], renv_o, out_sem.at[2])
-
+
+    y, z = lax.rem(me, SIDE), me // SIDE
+    layers = n // SIDE
+    above = lax.rem(z + 1, layers) * SIDE + y
+    below = lax.rem(z + layers - 1, layers) * SIDE + y
     barrier = pltpu.get_barrier_semaphore()
 
-    def greet(d, _):
-        pl.semaphore_signal(
-            barrier, inc=1, device_id={"blk": lax.rem(me + d, n)}, device_id_type=MESH
-        )
-        return 0
-
-    lax.fori_loop(1, n, greet, 0)
+    def greet(**device):
+        pl.semaphore_signal(barrier, inc=1, device_id=device, device_id_type=MESH)
+
+    for d in range(1, SIDE):
+        greet(blk=z * SIDE + lax.rem(y + d, SIDE))
+    greet(blk=above)
+    greet(blk=below)
     for d in (1, nseg - 1):
-        pl.semaphore_signal(
-            barrier, inc=1, device_id={"seg": lax.rem(seg + d, nseg)}, device_id_type=MESH
-        )
-
-    @pl.when(seg == 0)
+        greet(seg=lax.rem(seg + d, nseg))
+
+    @pl.when(y == SIDE - 1)
     def _():
-        own_left.start()
-
-    @pl.when(seg == nseg - 1)
+        greet(blk=right)
+
+    @pl.when(y == 0)
     def _():
-        own_right.start()
+        greet(blk=left)
+
+    ends = jnp.where(y == SIDE - 1, 1, 0) + jnp.where(y == 0, 1, 0)
+
+    def everyone():
+        for _ in range(layers // 2):
+            for which, other in ((0, above), (1, below)):
+                pl.semaphore_signal(
+                    ready.at[which], inc=1, device_id={"blk": other}, device_id_type=MESH
+                )
+            for which in (0, 1):
+                pl.semaphore_wait(ready.at[which], 1)
 
     loads[0].wait()
     live_rows, live_cols = dims[0, 0], dims[0, 1]
@@ -122,23 +134,18 @@
         )
 
     loads[1].wait()
-    zero_sum = jnp.zeros((8, half), F32)
-
-    def first(h):
-        def step(i, weight):
+
+    for h in (0, 1):
+
+        def step(i, _):
             row0 = pl.multiple_of(i * ROWS, ROWS)
             rows = pl.ds(row0, ROWS)
-            c = jnp.where(live(row0, h, ROWS), gv[rows, hs[h]].astype(F32), 0.0)
-            cb[h, rows] = c.astype(BF16)
-            return weight + fold(c * c)
-
-        return step
-
-    weight0 = zero_sum
-    for h in (0, 1):
-        weight0 = lax.fori_loop(0, width // ROWS, first(h), weight0)
-
-    pl.semaphore_wait(barrier, n - 1 + 2)
+            cb[h, rows] = jnp.where(live(row0, h, ROWS), gv[rows, hs[h]], jnp.zeros((), BF16))
+            return 0
+
+        lax.fori_loop(0, width // ROWS, step, 0)
+
+    pl.semaphore_wait(barrier, SIDE - 1 + 4 + ends)
     for h in (0, 1):
         for rc in (0, 1):
             x_copy(0, h, rc).start()
@@ -160,10 +167,11 @@
             cs[h] = dot(rm[...], hrc[h]).astype(BF16)
             c_copy(par, h).start()
 
+    def products(k):
+        for h in (0, 1):
+            pp[:, pl.ds(k * width + h * half, half)] = dot(lv[k], cb[h]).astype(BF16)
+
     def onsite():
-        for k in (0, 1):
-            for h in (0, 1):
-                pp[:, pl.ds(k * width + h * half, half)] = dot(lv[k], cb[h]).astype(BF16)
         for h in (0, 1):
             acc[h] = dot(pp[...], rv[:, hs[h]])
 
@@ -176,23 +184,38 @@
 
     lane = lax.broadcasted_iota(jnp.int32, (1, 128), 1)
 
-    def first_half(par, f, corr, weight, cross):
+    def field_sums():
+        sums = (jnp.zeros((8, half), F32),) * 3
+        for h in (0, 1):
+
+            def step(i, sums):
+                corr, weight, cross = sums
+                rows = pl.ds(pl.multiple_of(i * ROWS, ROWS), ROWS)
+                c = cb[h, rows].astype(F32)
+                return (
+                    corr + fold(vec[h, rows] * c),
+                    weight + fold(c * c),
+                    cross + fold(img[h, rows] * c),
+                )
+
+            sums = lax.fori_loop(0, width // ROWS, step, sums)
+        row = jnp.zeros((1, 128), F32)
+        for k in range(3):
+            row = jnp.where(lane == k, total(sums[k]), row)
+        return row
+
+    def first_half(par, f, row):
         x_whole(par, f).wait_recv()
         qq[...] = dot(hl[...], xr[par, f]).astype(BF16)
+        curv = jnp.zeros((8, half), F32)
+        for h in (0, 1):
+            part = dot_nt(qq[...], hrc[f, hs[h]])
+            local = acc[h]
+            curv = curv + fold(cb[h].astype(F32) * (local + 2.0 * part))
+            acc[h] = local + part
         c_copy(par, 1 - f).wait_recv()
-        curv = jnp.zeros((8, half), F32)
-        for h in (f, 1 - f):
-            part = dot_nt(qq[...], hrc[f, pl.ds(h * half, half)])
-            local = acc[h]
-            terms = local + 2.0 * part
-            if h is not f:
-                terms = terms + 2.0 * cr[par, h].astype(F32)
-            curv = curv + fold(cb[h].astype(F32) * terms)
-            acc[h] = local + part
-        sums = [total(s) for s in (corr, weight, cross, curv)]
-        row = jnp.zeros((1, 128), F32)
-        for k in range(4):
-            row = jnp.where(lane == k, sums[k], row)
+        curv = curv + 2.0 * fold(cb[1 - f].astype(F32) * cr[par, 1 - f].astype(F32))
+        row = jnp.where(lane == 3, total(curv), row)
         arsrc[par, 0:1] = row
         arbuf[par, n - 1 : n] = row
         for d in range(1, n):
@@ -266,30 +289,23 @@
                 diag[h, pl.ds(b, 128)] = jnp.where(live(b, h, 128), value, OUTSIDE)
 
     def update(par, f, last, a, scale, energy):
-        sums = (zero_sum, zero_sum, zero_sum)
         for h in (1 - f, f):
             if h is f:
                 c_copy(par, f).wait_recv()
 
-            def chunk(rc, sums, h=h):
-                def step(i, sums):
-                    corr, weight, cross = sums
+            def chunk(rc, _, h=h):
+                def step(i, _):
                     rows = pl.ds(pl.multiple_of(rc * half + i * ROWS, ROWS), ROWS)
                     c = cb[h, rows].astype(F32)
                     v = a * vec[h, rows] + scale * c
                     m = a * img[h, rows] + scale * (acc[h, rows] + cr[par, h, rows].astype(F32))
                     vec[h, rows] = v
                     img[h, rows] = m
-                    d = diag[h, rows]
-                    w = 1.0 + jnp.abs(d - energy)
-                    inv = pl.reciprocal(w, approx=True)
-                    inv = inv * (2.0 - w * inv)
-                    new = jnp.where(d < OUTSIDE, (m - energy * v) * inv, 0.0).astype(BF16)
-                    cb[h, rows] = new
-                    c = new.astype(F32)
-                    return corr + fold(v * c), weight + fold(c * c), cross + fold(m * c)
-
-                sums = lax.fori_loop(0, steps, step, sums)
+                    inv = pl.reciprocal(1.0 + jnp.abs(diag[h, rows] - energy), approx=True)
+                    cb[h, rows] = ((m - energy * v) * inv).astype(BF16)
+                    return 0
+
+                lax.fori_loop(0, steps, step, 0)
                 if h is not f:
                     x_copy(1 - par, h, rc).start()
                 else:
@@ -298,18 +314,16 @@
                     def _():
                         x_copy(1 - par, h, rc).start()
 
-                return sums
-
-            sums = lax.fori_loop(0, 2, chunk, sums)
-        return sums
+                return 0
+
+            lax.fori_loop(0, 2, chunk, 0)
 
     couple(0, (1, 0))
     loads[5].wait()
     loads[6].wait()
     prepare()
 
-    def iteration(t, carry):
-        energy, corr, weight, cross = carry
+    def iteration(t, energy):
         par = lax.rem(t, 2)
         f = par
 
@@ -319,26 +333,34 @@
                 c_copy(0, h).wait_send()
             couple(par, (1 - f, f))
 
+        products(0)
+        products(1)
         onsite()
-        first_half(par, f, corr, weight, cross)
+        row = field_sums()
+
+        @pl.when(t == 0)
+        def _():
+            everyone()
+
+        first_half(par, f, row)
         second_half(par, f)
         a, scale, energy = coefficients(par, t == 0, energy)
         for h in (0, 1):
             x_whole(0, h).wait_send()
-        return (energy,) + update(par, f, t == ITERS - 1, a, scale, energy)
-
-    carry = (jnp.zeros((1, 1), F32), zero_sum, weight0, zero_sum)
-    energy, corr, weight, cross = lax.fori_loop(0, ITERS, iteration, carry)
+        update(par, f, t == ITERS - 1, a, scale, energy)
+        return energy
+
+    energy = lax.fori_loop(0, ITERS, iteration, jnp.zeros((1, 1), F32))
     par = ITERS % 2
     f = par
     for h in (0, 1):
         c_copy(0, h).wait_send()
     couple(par, (1 - f,))
-    onsite()
+    products(0)
 
     loads[7].wait()
     size = kept[0, 0]
-    quarters = ((0, 0), (1, 0), (1, 1))
+    blocks = [(r, h) for r in range(width // 128) for h in range(r + 1)]
 
     def env_copy(which, part):
         src, dst = ((lsend, lrecv), (rsend, rrecv))[which]
@@ -361,6 +383,15 @@
     sends = (seg < nseg - 1, seg > 0)
     i = lax.broadcasted_iota(jnp.int32, (half, half), 0)
     j = lax.broadcasted_iota(jnp.int32, (half, half), 1)
+
+    def put(send, part, r, h, x):
+        x = jnp.where((i + r * half < size) & (j + h * half < size), x, 0.0).astype(BF16)
+        for q, (row, col) in enumerate(blocks):
+            if row // 2 == r and col // 2 == h:
+                b, c = row % 2 * 128, col % 2 * 128
+                send[part, q] = x[b : b + 128, c : c + 128]
+
+    quarters = ((0, 0), (1, 0), (1, 1))
     first, second = pl.ds(0, width), pl.ds(width, width)
     for h in (0, 1):
         ff[:, hs[h]] = cb[h]
@@ -377,25 +408,24 @@
     for part, (ours, theirs) in enumerate(
         ((second, first), (everything, everything), (first, second))
     ):
-        for q, (r, h) in enumerate(quarters):
-            mask = (i + r * half < size) & (j + h * half < size)
-            x = dot(tt[hs[r], ours], xx[theirs, hs[h]])
-            lsend[part, q] = jnp.where(mask, x, 0.0).astype(BF16)
+        for r, h in quarters:
+            put(lsend, part, r, h, dot(tt[hs[r], ours], xx[theirs, hs[h]]))
 
         @pl.when(sends[0])
         def _():
             env_copy(0, part).start()
 
-        for q, (r, h) in enumerate(quarters):
-            mask = (i + r * half < size) & (j + h * half < size)
-            x = dot_nt(yy[hs[r], theirs], ff[hs[h], ours])
-            rsend[part, q] = jnp.where(mask, x, 0.0).astype(BF16)
+        for r, h in quarters:
+            put(rsend, part, r, h, dot_nt(yy[hs[r], theirs], ff[hs[h], ours]))
 
         @pl.when(sends[1])
         def _():
             env_copy(1, part).start()
 
-    first_half(par, f, corr, weight, cross)
+    products(1)
+    onsite()
+    row = field_sums()
+    first_half(par, f, row)
     a, scale, energy = coefficients(par, None, energy)
     ratio[...] = jnp.broadcast_to(jnp.where(lane == 0, a, scale), (8, 128))
     for which in (0, 1):
@@ -415,28 +445,12 @@
 
         lax.fori_loop(0, width // ROWS, step, 0)
 
-    handoff = n * width * math.sqrt(width)
-
-    def combine(which, got, out):
-        env_copy(which, None).wait_recv()
-        ratio_copy(which).wait_recv()
-        row = ratio_in[which, 0:1]
-        a = jnp.sum(jnp.where(lane == 0, row, 0.0), axis=1, keepdims=True)
-        b = jnp.sum(jnp.where(lane == 1, row, 0.0), axis=1, keepdims=True)
-        weights = (handoff * a * a, handoff * a * b, handoff * b * b)
-        for q, (r, h) in enumerate(quarters):
-            x = sum(weights[part] * got[part, q].astype(F32) for part in range(3))
-            out[hs[r], hs[h]] = x.astype(BF16)
-            if r != h:
-                out[hs[h], hs[r]] = x.T.astype(BF16)
-
-    @pl.when(seg > 0)
-    def _():
-        combine(0, lrecv, lenv_o)
-
-    @pl.when(seg < nseg - 1)
-    def _():
-        combine(1, rrecv, renv_o)
+    for which, receives in ((0, seg > 0), (1, seg < nseg - 1)):
+
+        @pl.when(receives)
+        def _():
+            env_copy(which, None).wait_recv()
+            ratio_copy(which).wait_recv()
 
     x_whole(0, f).wait_send()
     c_copy(0, 1 - f).wait_send()
@@ -447,25 +461,46 @@
             env_copy(which, None).wait_send()
             ratio_copy(which).wait_send()
 
-    @pl.when(seg == 0)
-    def _():
-        own_left.wait()
-
-    @pl.when(seg == nseg - 1)
-    def _():
-        own_right.wait()
-
-
-def store(ground, energy, lenv, renv, ground_o, energy_o, lenv_o, renv_o, sem):
-    copies = [
-        pltpu.make_async_copy(src, dst.at[0, 0], sem.at[i])
-        for i, (src, dst) in enumerate(((ground, ground_o), (lenv, lenv_o), (renv, renv_o)))
-    ]
-    for copy in copies:
-        copy.start()
+
+def store(
+    n, nseg, width,
+    ground, energy, lrecv, rrecv, ratio_in, left_h, right_h,
+    ground_o, energy_o, lenv_o, renv_o, lb, rb, sem,
+):
+    seg = lax.axis_index("seg")
+    out = pltpu.make_async_copy(ground, ground_o.at[0, 0], sem.at[0])
+    out.start()
     energy_o[0] = energy[0, 0]
-    for copy in copies:
-        copy.wait()
+    handoff = n * width * math.sqrt(width)
+    lane = lax.broadcasted_iota(jnp.int32, (1, 128), 1)
+    blocks = [(r, h) for r in range(width // 128) for h in range(r + 1)]
+    sides = (
+        (seg == 0, left_h.at[0], lrecv, lb, lenv_o),
+        (seg == nseg - 1, right_h.at[pl.ds(0, width)], rrecv, rb, renv_o),
+    )
+    for which, (edge, own, got, made, dst) in enumerate(sides):
+
+        @pl.when(edge)
+        def _():
+            pltpu.make_async_copy(own, dst.at[0, 0], sem.at[1 + which]).start()
+
+        @pl.when(jnp.logical_not(edge))
+        def _():
+            row = ratio_in[which, 0:1]
+            a = jnp.sum(jnp.where(lane == 0, row, 0.0), axis=1, keepdims=True)
+            b = jnp.sum(jnp.where(lane == 1, row, 0.0), axis=1, keepdims=True)
+            weights = (handoff * a * a, handoff * a * b, handoff * b * b)
+            for q, (r, h) in enumerate(blocks):
+                x = sum(weights[part] * got[part, q].astype(F32) for part in range(3))
+                rows, cols = pl.ds(r * 128, 128), pl.ds(h * 128, 128)
+                made[rows, cols] = x.astype(BF16)
+                if r != h:
+                    made[cols, rows] = x.T.astype(BF16)
+            pltpu.make_async_copy(made, dst.at[0, 0], sem.at[1 + which]).start()
+
+    out.wait()
+    for which, (edge, own, got, made, dst) in enumerate(sides):
+        pltpu.make_async_copy(made, dst.at[0, 0], sem.at[1 + which]).wait()
 
 
 def per_device(
@@ -475,7 +510,8 @@
     width = guess_blocks.shape[-1]
     half = width // 2
     square, halves = (width, width), (2, width, half)
-    forms = (3, 3, half, half)
+    count = (width // 128) * (width // 128 + 1) // 2
+    forms = (3, count, 128, 128)
     hbm = pl.BlockSpec(memory_space=pltpu.HBM)
     vmem = pl.BlockSpec(memory_space=pltpu.VMEM)
     any_space = pl.BlockSpec(memory_space=pl.ANY)
@@ -505,53 +541,53 @@
         pltpu.VMEM((width, 2 * width), BF16),
         pltpu.VMEM(forms, BF16),
         pltpu.VMEM(forms, BF16),
-        pltpu.VMEM(forms, BF16),
-        pltpu.VMEM(forms, BF16),
         pltpu.VMEM((8, 128), F32),
-        pltpu.VMEM((2, 8, 128), F32),
         pltpu.VMEM((2, 8, 128), F32),
         pltpu.VMEM((2, n, 128), F32),
         pltpu.SMEM((1, 2), jnp.int32),
         pltpu.SMEM((1, 1), jnp.int32),
         dma((8,)), dma((2,)), dma((2, 2)), dma((2,)), dma((2, 2)), dma((2,)), dma((2,)),
-        dma((3,)), dma((2,)), dma((2,)), dma((2,)), dma((2,)),
+        dma((2,)), dma((2,)), dma((2,)), dma((2,)),
+        pltpu.SemaphoreType.REGULAR((2,)),
     ]
+    left, right = onsite_left[0, 0], onsite_right[0, 0].reshape(2 * width, width)
     results = pl.pallas_call(
         functools.partial(kernel, n, nseg, width),
         out_shape=(
             pltpu.VMEM(square, F32),
             pltpu.VMEM((8, 128), F32),
-            pltpu.VMEM(square, BF16),
-            pltpu.VMEM(square, BF16),
+            pltpu.VMEM(forms, BF16),
+            pltpu.VMEM(forms, BF16),
+            pltpu.VMEM((2, 8, 128), F32),
         ),
         in_specs=[hbm] * 7,
-        out_specs=(vmem,) * 4,
+        out_specs=(vmem,) * 5,
         scratch_shapes=scratch,
         compiler_params=pltpu.CompilerParams(
             collective_id=0, has_side_effects=True, vmem_limit_bytes=58 * 2**20
         ),
     )(
         guess_blocks[0, 0],
-        onsite_left[0, 0],
-        onsite_right[0, 0].reshape(2 * width, width),
+        left,
+        right,
         hopping_left[0, 0],
         hopping_right[0, 0],
         sector_dims[0],
         kept_dims,
     )
     return pl.pallas_call(
-        store,
+        functools.partial(store, n, nseg, width),
         out_shape=(
             jax.ShapeDtypeStruct((1, 1) + square, F32),
             jax.ShapeDtypeStruct((1,), F32),
             jax.ShapeDtypeStruct((1, 1) + square, BF16),
             jax.ShapeDtypeStruct((1, 1) + square, BF16),
         ),
-        in_specs=[vmem] * 4,
+        in_specs=[vmem] * 5 + [any_space] * 2,
         out_specs=(any_space, smem, any_space, any_space),
-        scratch_shapes=[dma((3,))],
-        compiler_params=pltpu.CompilerParams(vmem_limit_bytes=2**20),
-    )(*results)
+        scratch_shapes=[pltpu.VMEM(square, BF16), pltpu.VMEM(square, BF16), dma((3,))],
+        compiler_params=pltpu.CompilerParams(vmem_limit_bytes=4 * 2**20),
+    )(*results, left, right)
 
 
 def solution(mesh):

time: 98.8 us -> 94.2 us (0.953)
  Pallas kernels: 97.4 us -> 92.8 us
    pallas_call x1, Pallas kernels: 95.6 us -> 90.8 us  [per_device(): pl.pallas_call(functools.partial(kernel, n, nseg, width), out_shape=(pltp...]
where the time goes in v3:
time: 94.2 us; the launch traced here: 94.1 us
  Pallas kernels  92.8 us (99%)
  between operations  1.32 us (1%)
    pallas_call x1, Pallas kernels, per_device(): pl.pallas_call(functools.partial(kernel, n, nseg, width), out_shape=(pltp...  90.8 us
    pallas_call x1, Pallas kernels, per_device(): pl.pallas_call(functools.partial(store, n, nseg, width), out_shape=(jax.S...  2 us

profile of v3, /device:TPU:1, one launch (start us, length us, event | category | flops | bytes accessed | tf_op | source)
XLA Modules:
  0.0 94.1 jit_solution(8544644016103704640)
XLA Ops:
  1.3 0.0 copy-start
  1.3 0.0 copy-start.1
  1.3 90.8 %shard_map.102 = (f32[512,512]{1,0:T(8,128)S(1)}, f32[8,128]{1,0:T(8,128)S(1)}, bf16[3,10,128,128]{3,2,1,0:T(8,128)(2,1)S(1)}, bf16[3,10,128,128]{3,2,1,0:T(8,128)(2,1)S(1)}, f32[2,8,128]{2,1,0:T(8,128)S(1)}) custom-call(bf16[512,512]{1,0:T(8,128)(2,1)} %bitcast.10, bf16[2,512,512]{2,1,0:T(8,128)(2,1)} %bitcast.6, bf16[1024,512]{1,0:T(8,128)(2,1)} %bitcast.8, ...), custom_call_target="tpu_custom_call" | custom-call | tf_op jit(solution)/shard_map/pallas_call | solution.py:554
  92.1 0.0 copy-done
  92.1 0.0 copy-done.1
  92.1 2.0 %shard_map.103 = (f32[1,1,512,512]{3,2,1,0:T(8,128)}, f32[1]{0:T(128)}, bf16[1,1,512,512]{3,2,1,0:T(8,128)(2,1)}, bf16[1,1,512,512]{3,2,1,0:T(8,128)(2,1)}) custom-call(f32[512,512]{1,0:T(8,128)S(1)} %get-tuple-element.9.ground, f32[8,128]{1,0:T(8,128)S(1)} %get-tuple-element.10.energy, bf16[3,10,128,128]{3,2,1,0:T(8,128)(2,1)S(1)} %get-tuple-element.11.lrecv, ...), custom_call_target="tpu_custom_call" | custom-call | tf_op jit(solution)/shard_map/pallas_call | solution.py:578
Async XLA Ops:
  1.3 90.8 %copy-start = (bf16[1,1,2,512,512]{4,3,2,1,0:T(8,128)(2,1)S(1)}, bf16[1,1,2,512,512]{4,3,2,1,0:T(8,128)(2,1)}, u32[]{:S(2)}) copy-start(bf16[1,1,2,512,512]{4,3,2,1,0:T(8,128)(2,1)} %param.8) | copy-start | bytes 3145732
  1.3 90.8 %copy-start.1 = (bf16[1,1,2,512,512]{4,3,2,1,0:T(8,128)(2,1)S(1)}, bf16[1,1,2,512,512]{4,3,2,1,0:T(8,128)(2,1)}, u32[]{:S(2)}) copy-start(bf16[1,1,2,512,512]{4,3,2,1,0:T(8,128)(2,1)} %param.9) | copy-start | bytes 3145732

commit v4 on v3

--- a/solution.py
+++ b/solution.py
@@ -13,6 +13,7 @@
 F32 = jnp.float32
 BF16 = jnp.bfloat16
 SIDE = 4
+TILE = 256
 ROWS = 32
 OUTSIDE = 3e38
 
@@ -160,10 +161,23 @@
     loads[3].wait()
     loads[4].wait()
 
+    def c_tile(par, h, tile):
+        rows = pl.ds(tile * TILE, TILE)
+        return pltpu.make_async_remote_copy(
+            src_ref=cs.at[h, rows], dst_ref=cr.at[par, h, rows],
+            send_sem=cs_sem.at[h], recv_sem=cr_sem.at[par, h],
+            device_id={"blk": right}, device_id_type=MESH,
+        )
+
     def couple(par, halves):
-        for h in (0, 1):
-            rm[:, hs[h]] = dot(hlt[...], cb[h]).astype(BF16)
-        for h in halves:
+        first = halves[0]
+        for tile in range(width // TILE):
+            rows = pl.ds(tile * TILE, TILE)
+            for h in (0, 1):
+                rm[rows, hs[h]] = dot(hlt[rows, :], cb[h]).astype(BF16)
+            cs[first, rows] = dot(rm[rows, :], hrc[first]).astype(BF16)
+            c_tile(par, first, tile).start()
+        for h in halves[1:]:
             cs[h] = dot(rm[...], hrc[h]).astype(BF16)
             c_copy(par, h).start()
 
@@ -240,21 +254,21 @@
         )
         whole.wait_send()
         span = weight - corr * corr
-        length = jnp.sqrt(span)
-        off = (cross - corr * energy) / length
-        lower = (curv - 2.0 * corr * cross + corr * corr * energy) / span
+        inverse = 1.0 / span
+        slope = cross - corr * energy
+        lower = (curv - 2.0 * corr * cross + corr * corr * energy) * inverse
         gap = (energy - lower) / 2.0
-        radius = jnp.sqrt(gap * gap + off * off)
+        square = slope * slope * inverse
+        radius = jnp.sqrt(gap * gap + square)
         keep = radius - gap
-        turn = -off
-        norm = jnp.sqrt(keep * keep + turn * turn)
-        scale = turn / (length * norm)
-        a = keep / norm - scale * corr
+        inorm = lax.rsqrt(keep * keep + square)
+        scale = -slope * inverse * inorm
+        a = keep * inorm - scale * corr
         new = (energy + lower) / 2.0 - radius
         if start is None:
             return a, scale, new
         a = jnp.where(start, 0.0, a)
-        scale = jnp.where(start, 1.0 / length, scale)
+        scale = jnp.where(start, lax.rsqrt(weight), scale)
         new = jnp.where(start, lower, new)
         return a, scale, new
 
@@ -405,9 +419,8 @@
     for h in (0, 1):
         yy[:, pl.ds(width + h * half, half)] = dot(ff[:, first], rv[first, hs[h]]).astype(BF16)
     everything = pl.ds(0, 2 * width)
-    for part, (ours, theirs) in enumerate(
-        ((second, first), (everything, everything), (first, second))
-    ):
+    def form(part):
+        ours, theirs = ((second, first), (everything, everything), (first, second))[part]
         for r, h in quarters:
             put(lsend, part, r, h, dot(tt[hs[r], ours], xx[theirs, hs[h]]))
 
@@ -422,10 +435,13 @@
         def _():
             env_copy(1, part).start()
 
+    form(0)
+    form(1)
     products(1)
     onsite()
     row = field_sums()
     first_half(par, f, row)
+    form(2)
     a, scale, energy = coefficients(par, None, energy)
     ratio[...] = jnp.broadcast_to(jnp.where(lane == 0, a, scale), (8, 128))
     for which in (0, 1):

time: 94.2 us -> 93.7 us (level)
  no operation moved by 1% of the time
where the time goes in v4:
time: 93.7 us; the launch traced here: 93.6 us
  Pallas kernels  92.3 us (99%)
  between operations  1.32 us (1%)
    pallas_call x1, Pallas kernels, per_device(): pl.pallas_call(functools.partial(kernel, n, nseg, width), out_shape=(pltp...  90.3 us
    pallas_call x1, Pallas kernels, per_device(): pl.pallas_call(functools.partial(store, n, nseg, width), out_shape=(jax.S...  2 us

profile of v4, /device:TPU:1, one launch (start us, length us, event | category | flops | bytes accessed | tf_op | source)
XLA Modules:
  0.0 93.6 jit_solution(12680638604656729820)
XLA Ops:
  1.3 0.0 copy-start
  1.3 0.0 copy-start.1
  1.3 90.3 %shard_map.102 = (f32[512,512]{1,0:T(8,128)S(1)}, f32[8,128]{1,0:T(8,128)S(1)}, bf16[3,10,128,128]{3,2,1,0:T(8,128)(2,1)S(1)}, bf16[3,10,128,128]{3,2,1,0:T(8,128)(2,1)S(1)}, f32[2,8,128]{2,1,0:T(8,128)S(1)}) custom-call(bf16[512,512]{1,0:T(8,128)(2,1)} %bitcast.10, bf16[2,512,512]{2,1,0:T(8,128)(2,1)} %bitcast.6, bf16[1024,512]{1,0:T(8,128)(2,1)} %bitcast.8, ...), custom_call_target="tpu_custom_call" | custom-call | tf_op jit(solution)/shard_map/pallas_call | solution.py:570
  91.6 0.0 copy-done
  91.6 0.0 copy-done.1
  91.6 2.0 %shard_map.103 = (f32[1,1,512,512]{3,2,1,0:T(8,128)}, f32[1]{0:T(128)}, bf16[1,1,512,512]{3,2,1,0:T(8,128)(2,1)}, bf16[1,1,512,512]{3,2,1,0:T(8,128)(2,1)}) custom-call(f32[512,512]{1,0:T(8,128)S(1)} %get-tuple-element.9.ground, f32[8,128]{1,0:T(8,128)S(1)} %get-tuple-element.10.energy, bf16[3,10,128,128]{3,2,1,0:T(8,128)(2,1)S(1)} %get-tuple-element.11.lrecv, ...), custom_call_target="tpu_custom_call" | custom-call | tf_op jit(solution)/shard_map/pallas_call | solution.py:594
Async XLA Ops:
  1.3 90.3 %copy-start = (bf16[1,1,2,512,512]{4,3,2,1,0:T(8,128)(2,1)S(1)}, bf16[1,1,2,512,512]{4,3,2,1,0:T(8,128)(2,1)}, u32[]{:S(2)}) copy-start(bf16[1,1,2,512,512]{4,3,2,1,0:T(8,128)(2,1)} %param.8) | copy-start | bytes 3145732
  1.3 90.3 %copy-start.1 = (bf16[1,1,2,512,512]{4,3,2,1,0:T(8,128)(2,1)S(1)}, bf16[1,1,2,512,512]{4,3,2,1,0:T(8,128)(2,1)}, u32[]{:S(2)}) copy-start(bf16[1,1,2,512,512]{4,3,2,1,0:T(8,128)(2,1)} %param.9) | copy-start | bytes 3145732

commit v5 on v4

--- a/solution.py
+++ b/solution.py
@@ -14,7 +14,7 @@
 BF16 = jnp.bfloat16
 SIDE = 4
 TILE = 256
-ROWS = 32
+ROWS = 64
 OUTSIDE = 3e38
 
 

time: 93.7 us -> 92.9 us (level)
  no operation moved by 1% of the time
where the time goes in v5:
time: 92.9 us; the launch traced here: 92.8 us
  Pallas kernels  91.5 us (98%)
  between operations  1.32 us (1%)
    pallas_call x1, Pallas kernels, per_device(): pl.pallas_call(functools.partial(kernel, n, nseg, width), out_shape=(pltp...  89.5 us
    pallas_call x1, Pallas kernels, per_device(): pl.pallas_call(functools.partial(store, n, nseg, width), out_shape=(jax.S...  2 us

profile of v5, /device:TPU:1, one launch (start us, length us, event | category | flops | bytes accessed | tf_op | source)
XLA Modules:
  0.0 92.8 jit_solution(13027009294495226244)
XLA Ops:
  1.3 0.0 copy-start
  1.3 0.0 copy-start.1
  1.3 89.5 %shard_map.102 = (f32[512,512]{1,0:T(8,128)S(1)}, f32[8,128]{1,0:T(8,128)S(1)}, bf16[3,10,128,128]{3,2,1,0:T(8,128)(2,1)S(1)}, bf16[3,10,128,128]{3,2,1,0:T(8,128)(2,1)S(1)}, f32[2,8,128]{2,1,0:T(8,128)S(1)}) custom-call(bf16[512,512]{1,0:T(8,128)(2,1)} %bitcast.10, bf16[2,512,512]{2,1,0:T(8,128)(2,1)} %bitcast.6, bf16[1024,512]{1,0:T(8,128)(2,1)} %bitcast.8, ...), custom_call_target="tpu_custom_call" | custom-call | tf_op jit(solution)/shard_map/pallas_call | solution.py:570
  90.8 0.0 copy-done
  90.8 0.0 copy-done.1
  90.9 2.0 %shard_map.103 = (f32[1,1,512,512]{3,2,1,0:T(8,128)}, f32[1]{0:T(128)}, bf16[1,1,512,512]{3,2,1,0:T(8,128)(2,1)}, bf16[1,1,512,512]{3,2,1,0:T(8,128)(2,1)}) custom-call(f32[512,512]{1,0:T(8,128)S(1)} %get-tuple-element.9.ground, f32[8,128]{1,0:T(8,128)S(1)} %get-tuple-element.10.energy, bf16[3,10,128,128]{3,2,1,0:T(8,128)(2,1)S(1)} %get-tuple-element.11.lrecv, ...), custom_call_target="tpu_custom_call" | custom-call | tf_op jit(solution)/shard_map/pallas_call | solution.py:594
Async XLA Ops:
  1.3 89.6 %copy-start = (bf16[1,1,2,512,512]{4,3,2,1,0:T(8,128)(2,1)S(1)}, bf16[1,1,2,512,512]{4,3,2,1,0:T(8,128)(2,1)}, u32[]{:S(2)}) copy-start(bf16[1,1,2,512,512]{4,3,2,1,0:T(8,128)(2,1)} %param.8) | copy-start | bytes 3145732
  1.3 89.6 %copy-start.1 = (bf16[1,1,2,512,512]{4,3,2,1,0:T(8,128)(2,1)S(1)}, bf16[1,1,2,512,512]{4,3,2,1,0:T(8,128)(2,1)}, u32[]{:S(2)}) copy-start(bf16[1,1,2,512,512]{4,3,2,1,0:T(8,128)(2,1)} %param.9) | copy-start | bytes 3145732
